TPU v7x, 512 devices: a whole 4x8x8 slice. The times are simulated.
512 devices in a mesh: grid: 128 (over z, y, core), band: 4 (over x).
Axes of the slice: x: 4, y: 8, z: 8, core: 2. Of those that a mesh axis runs over, the one named last changes fastest.
Arguments:
- visibility: float32 [4, 16384, 2, 384], P('band', 'grid'), may hold values from -6 to 6
- weights: float32 [4, 16384, 384], P('band', 'grid'), may hold values from 0.2 to 2
- block_uv: float32 [16384, 2, 16], P('grid'), may hold values from -19 to 19
- chan_ratio: float32 [4, 24], P('band'), may hold values from 0.6 to 1
- block_subgrid: int32 [4, 16384], P('band', 'grid'), may hold values from 0 to 1023, as said below
- block_stations: int32 [16384, 2], P('grid'), may hold values from 0 to 127, as said below
- screens: bfloat16 [128, 64, 64], P('grid'), may hold values from 0.099609375 to 1.8984375
Outputs:
- subgrids: float32 [64, 1024, 128], P('band', 'grid')
Inputs may be any that keep to these rules, and one draw needn't show every extreme that they name: `block_subgrid`: global subgrid numbers; subgrid g is owned by grid index g // 8. In each band the 128 blocks of one grid index name one owner at most 2 times, and one owner, drawn from the seed, exactly 2 times from every grid index. `block_stations`: the two stations of a block differ.
All inputs are finite; a program needn't handle non-finite values.
Results may differ from a plain program's by a relative error of at most 0.0046.
Values may be sent and summed in bfloat16 or wider, within the bound.
No kernel may reach another device: no remote copies, remote signals or barrier semaphores. Data moves between devices by JAX's collectives and lax.ppermute only.
A program may use at most 64 MiB of HBM per device.

v0:
```python
import math

import jax
import jax.numpy as jnp
from jax import lax
from jax.sharding import PartitionSpec as P

SUB = 64
SG_DEV = 8


def phase_angles(coords, chan_scale, grid_side):
    blocks = coords.shape[0]
    vis_len = coords.shape[2] * chan_scale.shape[0]
    u_coord = (coords[:, 0, :, None] * chan_scale[None, None, :]).reshape(blocks, vis_len)
    v_coord = (coords[:, 1, :, None] * chan_scale[None, None, :]).reshape(blocks, vis_len)
    centred = jnp.arange(grid_side).astype(jnp.float32) - grid_side / 2
    factor = 2.0 * math.pi / grid_side
    across_phase = factor * u_coord[:, None, :] * centred[None, :, None]
    down_phase = factor * v_coord[:, :, None] * centred[None, None, :]
    return (across_phase, down_phase)


def image_blocks(weighted, coords, chan_scale, station_one, station_two, screen_table):
    grid_side = screen_table.shape[1]
    vis_len = weighted.shape[2]
    across_phase, down_phase = phase_angles(coords, chan_scale, grid_side)
    cos_across = jnp.cos(across_phase)
    sin_across = jnp.sin(across_phase)
    real_vis = weighted[:, 0, None, :]
    imag_vis = weighted[:, 1, None, :]
    left_rows = jnp.concatenate(
        [
            real_vis * cos_across - imag_vis * sin_across,
            real_vis * sin_across + imag_vis * cos_across,
        ],
        axis=1,
    ).astype(jnp.bfloat16)
    right_cols = jnp.concatenate([jnp.cos(down_phase), jnp.sin(down_phase)], axis=2).astype(
        jnp.bfloat16
    )
    products = jnp.einsum("gxk,gky->gxy", left_rows, right_cols, preferred_element_type=jnp.float32)
    real_img = (products[:, :grid_side, :grid_side] - products[:, grid_side:, grid_side:]) / vis_len
    imag_img = (products[:, :grid_side, grid_side:] + products[:, grid_side:, :grid_side]) / vis_len
    beam_gain = screen_table[station_one].astype(jnp.float32) * screen_table[station_two].astype(
        jnp.float32
    )
    return jnp.concatenate([beam_gain * real_img, beam_gain * imag_img], axis=2).astype(
        jnp.bfloat16
    )


def dft_parts(row_index, col_index, grid_side):
    phase = (row_index[:, None] * col_index[None, :] % grid_side).astype(jnp.float32) * (
        2.0 * math.pi / grid_side
    )
    norm = 1.0 / math.sqrt(grid_side)
    return (jnp.cos(phase) * norm, -jnp.sin(phase) * norm)


def shards(visibility, weights, block_uv, chan_ratio, block_subgrid, block_stations, screens):
    grid_count = lax.axis_size("grid")
    vis_rows = visibility[0]
    weight_rows = weights[0]
    targets = block_subgrid[0]
    chan_scale = chan_ratio[0]
    blocks = vis_rows.shape[0]
    capacity = 2 * blocks // grid_count
    slot_count = grid_count * capacity
    group_rows = 16
    screen_table = lax.all_gather(screens, "grid", axis=0, tiled=True)
    owner_dev = targets // SG_DEV
    local_index = targets % SG_DEV
    block_order = jnp.arange(blocks, dtype=jnp.int32)
    same_owner = (owner_dev[:, None] == owner_dev[None, :]) & (
        block_order[None, :] < block_order[:, None]
    )
    owner_rank = jnp.sum(same_owner.astype(jnp.int32), axis=1)
    position = owner_dev * capacity + owner_rank
    slot_range = jnp.arange(slot_count, dtype=jnp.int32)
    slot_hits = position[None, :] == slot_range[:, None]
    present = jnp.any(slot_hits, axis=1)
    source = jnp.sum(jnp.where(slot_hits, block_order[None, :], 0), axis=1)
    payload = vis_rows * weight_rows[:, None, :]
    payload = jnp.where(present[:, None, None], payload[source], 0.0)
    coords = jnp.where(present[:, None, None], block_uv[source], 0.0)
    block_tags = jnp.stack([local_index, block_stations[:, 0], block_stations[:, 1]], axis=1)[
        source
    ]
    empty_tag = jnp.array([-1, 0, 0], dtype=jnp.int32)
    block_tags = jnp.where(present[:, None], block_tags, empty_tag[None, :])
    arrived = (
        lax.all_to_all(
            payload.reshape((grid_count, capacity) + payload.shape[1:]),
            "grid",
            split_axis=0,
            concat_axis=0,
            tiled=True,
        ),
        lax.all_to_all(
            coords.reshape((grid_count, capacity) + coords.shape[1:]),
            "grid",
            split_axis=0,
            concat_axis=0,
            tiled=True,
        ),
        lax.all_to_all(
            block_tags.reshape(grid_count, capacity, 3),
            "grid",
            split_axis=0,
            concat_axis=0,
            tiled=True,
        ),
    )
    recv_payload = arrived[0].reshape((slot_count,) + arrived[0].shape[2:])
    recv_coords = arrived[1].reshape((slot_count,) + arrived[1].shape[2:])
    recv_tags = arrived[2].reshape(slot_count, 3)
    station_one = recv_tags[:, 1]
    station_two = recv_tags[:, 2]
    target = recv_tags[:, 0]
    partial_rows = SG_DEV
    turn_count = slot_count // group_rows

    def accumulate(turn_index, running):
        row_start = turn_index * group_rows
        image_stack = image_blocks(
            lax.dynamic_slice_in_dim(recv_payload, row_start, group_rows, 0),
            lax.dynamic_slice_in_dim(recv_coords, row_start, group_rows, 0),
            chan_scale,
            lax.dynamic_slice_in_dim(station_one, row_start, group_rows, 0),
            lax.dynamic_slice_in_dim(station_two, row_start, group_rows, 0),
            screen_table,
        )
        owners_now = lax.dynamic_slice_in_dim(target, row_start, group_rows, 0)
        selector = (
            owners_now[None, :] == jnp.arange(partial_rows, dtype=jnp.int32)[:, None]
        ).astype(jnp.bfloat16)
        return running + jnp.dot(
            selector,
            image_stack.reshape(group_rows, SUB * 2 * SUB),
            preferred_element_type=jnp.float32,
        )

    running = lax.fori_loop(
        0, turn_count, accumulate, jnp.zeros((partial_rows, SUB * 2 * SUB), jnp.float32)
    )
    incomplete_value = running.reshape(SG_DEV, SUB, 2 * SUB)
    pixel_index = jnp.arange(SUB, dtype=jnp.int32)
    taper_line = jnp.sin(math.pi * (pixel_index.astype(jnp.float32) + 0.5) / SUB)
    complete_window = taper_line[:, None] * jnp.concatenate([taper_line, taper_line])[None, :]
    cos_part, sin_part = dft_parts(pixel_index, pixel_index, SUB)
    column_matrix = jnp.concatenate(
        [
            jnp.concatenate([cos_part, sin_part], axis=1),
            jnp.concatenate([-sin_part, cos_part], axis=1),
        ],
        axis=0,
    )
    column_list = jnp.einsum(
        "ste,ep->stp",
        incomplete_value * complete_window[None],
        column_matrix,
        precision=lax.Precision.HIGHEST,
    )
    exchanged_rows = jnp.concatenate([-column_list[:, :, SUB:], column_list[:, :, :SUB]], axis=2)
    row_index = jnp.arange(SUB // lax.axis_size("band") * lax.axis_size("band"), dtype=jnp.int32)
    cosine_rows, sine_rows = dft_parts(row_index, pixel_index, SUB)
    leading_term = jnp.einsum(
        "ar,prw->apw", cosine_rows, column_list, precision=lax.Precision.HIGHEST
    )
    return lax.psum_scatter(
        leading_term
        + jnp.einsum("ar,prw->apw", sine_rows, exchanged_rows, precision=lax.Precision.HIGHEST),
        "band",
        scatter_dimension=0,
        tiled=True,
    )


def solution(mesh):
    in_specs = (
        P("band", "grid", None, None),
        P("band", "grid", None),
        P("grid", None, None),
        P("band", None),
        P("band", "grid"),
        P("grid", None),
        P("grid", None, None),
    )
    out_specs = P("band", "grid", None)
    return jax.shard_map(shards, mesh=mesh, in_specs=in_specs, out_specs=out_specs, check_vma=False)
```

profile of v0, /device:TPU:8, one launch (start us, length us, event | category | flops | bytes accessed | tf_op | source)
XLA Modules:
  0.0 564.2 jit_solution(4488002791718638419)
XLA Ops:
  12.9 17.4 %all-to-all-start = ((s32[128,2,3]{2,1,0:T(2,128)}), s32[128,2,3]{2,1,0:T(2,128)S(1)}, u32[]{:S(2)}, u32[]{:S(2)}) async-start(s32[128,2,3]{2,1,0:T(2,128)} %broadcast_select_fusion.2), calls=%async_computation | async-start | bytes 262144 | tf_op jit(solution)/shard_map/all_to_all | solution.py:107
  35.0 7.3 %all-to-all-done = s32[128,2,3]{2,1,0:T(2,128)S(1)} async-done(((s32[128,2,3]{2,1,0:T(2,128)}), s32[128,2,3]{2,1,0:T(2,128)S(1)}, u32[]{:S(2)}, u32[]{:S(2)}) %all-to-all-start) | async-done | bytes 3104 | tf_op jit(solution)/shard_map/all_to_all | solution.py:107
  42.2 6.5 %all-to-all-start.2 = ((f32[128,2,2,16]{3,1,2,0:T(2,128)}), f32[128,2,2,16]{3,1,2,0:T(2,128)S(1)}, u32[]{:S(2)}, u32[]{:S(2)}) async-start(f32[128,2,2,16]{3,1,2,0:T(2,128)} %copy.61), calls=%async_computation.2 | async-start | bytes 524288 | tf_op jit(solution)/shard_map/all_to_all | solution.py:100
  50.6 12.9 %all-to-all-done.2 = f32[128,2,2,16]{3,1,2,0:T(2,128)S(1)} async-done(((f32[128,2,2,16]{3,1,2,0:T(2,128)}), f32[128,2,2,16]{3,1,2,0:T(2,128)S(1)}, u32[]{:S(2)}, u32[]{:S(2)}) %all-to-all-start.2) | async-done | bytes 32800 | tf_op jit(solution)/shard_map/all_to_all | solution.py:100
  70.9 24.7 %all-to-all-done.1 = f32[128,2,2,384]{3,1,2,0:T(2,128)S(1)} async-done(((f32[128,2,2,384]{3,1,2,0:T(2,128)}), f32[128,2,2,384]{3,1,2,0:T(2,128)S(1)}, u32[]{:S(2)}, u32[]{:S(2)}) %all-to-all-start.1) | async-done | bytes 786464 | tf_op jit(solution)/shard_map/all_to_all | solution.py:93
  96.0 32.8 %all-gather.2.cloned.1.call-done = bf16[128,64,64]{2,1,0:T(8,128)(2,1)} async-done(((bf16[1,64,64]{2,1,0:T(8,128)(2,1)}), bf16[128,64,64]{2,1,0:T(8,128)(2,1)}) %all-gather.2.cloned.1.call-update) | async-done | bytes 1048592 | tf_op jit(solution)/shard_map/all_gather | solution.py:71
  128.8 401.1 %while.16 = (s32[]{:T(128)}, f32[8,8192]{1,0:T(8,128)S(1)}, s32[256]{0:T(256)S(1)}, s32[256]{0:T(256)S(1)}, bf16[128,64,64]{2,1,0:T(8,128)(2,1)}, /*index=5*/s32...) while((s32[]{:T(128)}, f32[8,8192]{1,0:T(8,128)S(1)}, ...), condition=%wide.region_4.5_spmd.clone, body=%wide.region_3.4_spmd.clone.sunk | while | flops 215837024 | bytes 11310849 | solution.py:144
  135.5 11.8 %fusion.78 = (bf16[16,384,64]{2,1,0:T(8,128)(2,1)S(1)}, bf16[16,384,64]{2,1,0:T(8,128)(2,1)S(1)}) fusion(f32[64]{0:T(128)S(1)} %convert_add_fusion.2, f32[16,384]{1,0:T(8,128)S(1)} %get-tuple-element.395), kind=kLoop, calls=%fused_computation.8.clone.1 | loop fusion | flops 1179648 | bytes 1597696 | tf_op jit(solution)/shard_map/convert.2
  160.6 11.8 %fusion.78 = (bf16[16,384,64]{2,1,0:T(8,128)(2,1)S(1)}, bf16[16,384,64]{2,1,0:T(8,128)(2,1)S(1)}) fusion(f32[64]{0:T(128)S(1)} %convert_add_fusion.2, f32[16,384]{1,0:T(8,128)S(1)} %get-tuple-element.395), kind=kLoop, calls=%fused_computation.8.clone.1 | loop fusion | flops 1179648 | bytes 1597696 | tf_op jit(solution)/shard_map/convert.2
  185.7 11.8 %fusion.78 = (bf16[16,384,64]{2,1,0:T(8,128)(2,1)S(1)}, bf16[16,384,64]{2,1,0:T(8,128)(2,1)S(1)}) fusion(f32[64]{0:T(128)S(1)} %convert_add_fusion.2, f32[16,384]{1,0:T(8,128)S(1)} %get-tuple-element.395), kind=kLoop, calls=%fused_computation.8.clone.1 | loop fusion | flops 1179648 | bytes 1597696 | tf_op jit(solution)/shard_map/convert.2
  210.7 11.8 %fusion.78 = (bf16[16,384,64]{2,1,0:T(8,128)(2,1)S(1)}, bf16[16,384,64]{2,1,0:T(8,128)(2,1)S(1)}) fusion(f32[64]{0:T(128)S(1)} %convert_add_fusion.2, f32[16,384]{1,0:T(8,128)S(1)} %get-tuple-element.395), kind=kLoop, calls=%fused_computation.8.clone.1 | loop fusion | flops 1179648 | bytes 1597696 | tf_op jit(solution)/shard_map/convert.2
  235.8 11.8 %fusion.78 = (bf16[16,384,64]{2,1,0:T(8,128)(2,1)S(1)}, bf16[16,384,64]{2,1,0:T(8,128)(2,1)S(1)}) fusion(f32[64]{0:T(128)S(1)} %convert_add_fusion.2, f32[16,384]{1,0:T(8,128)S(1)} %get-tuple-element.395), kind=kLoop, calls=%fused_computation.8.clone.1 | loop fusion | flops 1179648 | bytes 1597696 | tf_op jit(solution)/shard_map/convert.2
  260.9 11.8 %fusion.78 = (bf16[16,384,64]{2,1,0:T(8,128)(2,1)S(1)}, bf16[16,384,64]{2,1,0:T(8,128)(2,1)S(1)}) fusion(f32[64]{0:T(128)S(1)} %convert_add_fusion.2, f32[16,384]{1,0:T(8,128)S(1)} %get-tuple-element.395), kind=kLoop, calls=%fused_computation.8.clone.1 | loop fusion | flops 1179648 | bytes 1597696 | tf_op jit(solution)/shard_map/convert.2
  285.9 11.8 %fusion.78 = (bf16[16,384,64]{2,1,0:T(8,128)(2,1)S(1)}, bf16[16,384,64]{2,1,0:T(8,128)(2,1)S(1)}) fusion(f32[64]{0:T(128)S(1)} %convert_add_fusion.2, f32[16,384]{1,0:T(8,128)S(1)} %get-tuple-element.395), kind=kLoop, calls=%fused_computation.8.clone.1 | loop fusion | flops 1179648 | bytes 1597696 | tf_op jit(solution)/shard_map/convert.2
  311.0 11.8 %fusion.78 = (bf16[16,384,64]{2,1,0:T(8,128)(2,1)S(1)}, bf16[16,384,64]{2,1,0:T(8,128)(2,1)S(1)}) fusion(f32[64]{0:T(128)S(1)} %convert_add_fusion.2, f32[16,384]{1,0:T(8,128)S(1)} %get-tuple-element.395), kind=kLoop, calls=%fused_computation.8.clone.1 | loop fusion | flops 1179648 | bytes 1597696 | tf_op jit(solution)/shard_map/convert.2
  336.1 11.8 %fusion.78 = (bf16[16,384,64]{2,1,0:T(8,128)(2,1)S(1)}, bf16[16,384,64]{2,1,0:T(8,128)(2,1)S(1)}) fusion(f32[64]{0:T(128)S(1)} %convert_add_fusion.2, f32[16,384]{1,0:T(8,128)S(1)} %get-tuple-element.395), kind=kLoop, calls=%fused_computation.8.clone.1 | loop fusion | flops 1179648 | bytes 1597696 | tf_op jit(solution)/shard_map/convert.2
  361.2 11.8 %fusion.78 = (bf16[16,384,64]{2,1,0:T(8,128)(2,1)S(1)}, bf16[16,384,64]{2,1,0:T(8,128)(2,1)S(1)}) fusion(f32[64]{0:T(128)S(1)} %convert_add_fusion.2, f32[16,384]{1,0:T(8,128)S(1)} %get-tuple-element.395), kind=kLoop, calls=%fused_computation.8.clone.1 | loop fusion | flops 1179648 | bytes 1597696 | tf_op jit(solution)/shard_map/convert.2
  386.2 11.8 %fusion.78 = (bf16[16,384,64]{2,1,0:T(8,128)(2,1)S(1)}, bf16[16,384,64]{2,1,0:T(8,128)(2,1)S(1)}) fusion(f32[64]{0:T(128)S(1)} %convert_add_fusion.2, f32[16,384]{1,0:T(8,128)S(1)} %get-tuple-element.395), kind=kLoop, calls=%fused_computation.8.clone.1 | loop fusion | flops 1179648 | bytes 1597696 | tf_op jit(solution)/shard_map/convert.2
  411.3 11.8 %fusion.78 = (bf16[16,384,64]{2,1,0:T(8,128)(2,1)S(1)}, bf16[16,384,64]{2,1,0:T(8,128)(2,1)S(1)}) fusion(f32[64]{0:T(128)S(1)} %convert_add_fusion.2, f32[16,384]{1,0:T(8,128)S(1)} %get-tuple-element.395), kind=kLoop, calls=%fused_computation.8.clone.1 | loop fusion | flops 1179648 | bytes 1597696 | tf_op jit(solution)/shard_map/convert.2
  436.4 11.8 %fusion.78 = (bf16[16,384,64]{2,1,0:T(8,128)(2,1)S(1)}, bf16[16,384,64]{2,1,0:T(8,128)(2,1)S(1)}) fusion(f32[64]{0:T(128)S(1)} %convert_add_fusion.2, f32[16,384]{1,0:T(8,128)S(1)} %get-tuple-element.395), kind=kLoop, calls=%fused_computation.8.clone.1 | loop fusion | flops 1179648 | bytes 1597696 | tf_op jit(solution)/shard_map/convert.2
  461.4 11.8 %fusion.78 = (bf16[16,384,64]{2,1,0:T(8,128)(2,1)S(1)}, bf16[16,384,64]{2,1,0:T(8,128)(2,1)S(1)}) fusion(f32[64]{0:T(128)S(1)} %convert_add_fusion.2, f32[16,384]{1,0:T(8,128)S(1)} %get-tuple-element.395), kind=kLoop, calls=%fused_computation.8.clone.1 | loop fusion | flops 1179648 | bytes 1597696 | tf_op jit(solution)/shard_map/convert.2
  486.5 11.8 %fusion.78 = (bf16[16,384,64]{2,1,0:T(8,128)(2,1)S(1)}, bf16[16,384,64]{2,1,0:T(8,128)(2,1)S(1)}) fusion(f32[64]{0:T(128)S(1)} %convert_add_fusion.2, f32[16,384]{1,0:T(8,128)S(1)} %get-tuple-element.395), kind=kLoop, calls=%fused_computation.8.clone.1 | loop fusion | flops 1179648 | bytes 1597696 | tf_op jit(solution)/shard_map/convert.2
  511.6 11.8 %fusion.78 = (bf16[16,384,64]{2,1,0:T(8,128)(2,1)S(1)}, bf16[16,384,64]{2,1,0:T(8,128)(2,1)S(1)}) fusion(f32[64]{0:T(128)S(1)} %convert_add_fusion.2, f32[16,384]{1,0:T(8,128)S(1)} %get-tuple-element.395), kind=kLoop, calls=%fused_computation.8.clone.1 | loop fusion | flops 1179648 | bytes 1597696 | tf_op jit(solution)/shard_map/convert.2
  532.3 23.6 %reduce-scatter.2.cloned.1.call-done = f32[16,8,128]{2,0,1:T(8,128)} async-done(((f32[64,8,128]{2,0,1:T(8,128)}), f32[16,8,128]{2,0,1:T(8,128)}) %reduce-scatter.2.cloned.1.call-update) | async-done | bytes 65552 | tf_op jit(solution)/shard_map/reduce_scatter | solution.py:171
  (405 shorter events, 234.6 us)
Async XLA Ops:
  6.5 24.5 %copy-start.1 = (f32[1,128,384]{2,1,0:T(8,128)S(1)}, f32[1,128,384]{2,1,0:T(8,128)}, u32[]{:S(2)}) copy-start(f32[1,128,384]{2,1,0:T(8,128)} %param.11) | copy-start | bytes 589828
  6.5 24.5 %copy-start = (f32[1,128,2,384]{3,2,1,0:T(2,128)S(1)}, f32[1,128,2,384]{3,2,1,0:T(2,128)}, u32[]{:S(2)}) copy-start(f32[1,128,2,384]{3,2,1,0:T(2,128)} %param.10) | copy-start | bytes 1179652
  6.5 24.7 %copy-start.2 = (f32[128,2,16]{0,2,1:T(8,128)S(1)}, f32[128,2,16]{0,2,1:T(8,128)}, u32[]{:S(2)}) copy-start(f32[128,2,16]{0,2,1:T(8,128)} %param.12) | copy-start | bytes 49156
  12.9 29.3 %all-to-all-start = ((s32[128,2,3]{2,1,0:T(2,128)}), s32[128,2,3]{2,1,0:T(2,128)S(1)}, u32[]{:S(2)}, u32[]{:S(2)}) async-start(s32[128,2,3]{2,1,0:T(2,128)} %broadcast_select_fusion.2), calls=%async_computation | async-start | bytes 262144 | tf_op jit(solution)/shard_map/all_to_all | solution.py:107
  30.3 98.5 %all-gather.2.cloned.1.call-start = ((), (), s32[]{:S(2)}) async-start(), calls=%async_computation.4 | async-start | bytes 2113536 | tf_op jit(solution)/shard_map/all_gather | solution.py:71
  42.2 21.3 %all-to-all-start.2 = ((f32[128,2,2,16]{3,1,2,0:T(2,128)}), f32[128,2,2,16]{3,1,2,0:T(2,128)S(1)}, u32[]{:S(2)}, u32[]{:S(2)}) async-start(f32[128,2,2,16]{3,1,2,0:T(2,128)} %copy.61), calls=%async_computation.2 | async-start | bytes 524288 | tf_op jit(solution)/shard_map/all_to_all | solution.py:100
  63.5 32.1 %all-to-all-start.1 = ((f32[128,2,2,384]{3,1,2,0:T(2,128)}), f32[128,2,2,384]{3,1,2,0:T(2,128)S(1)}, u32[]{:S(2)}, u32[]{:S(2)}) async-start(f32[128,2,2,384]{3,1,2,0:T(2,128)} %copy.57), calls=%async_computation.1 | async-start | bytes 1572864 | tf_op jit(solution)/shard_map/all_to_all | solution.py:93
  69.7 486.2 %reduce-scatter.2.cloned.1.call-start = ((), (), s32[]{:S(2)}) async-start(), calls=%async_computation.5 | async-start | bytes 327680 | tf_op jit(solution)/shard_map/reduce_scatter | solution.py:171
  70.4 58.4 %copy-start.3 = (f32[1,24]{1,0:T(1,128)S(1)}, f32[1,24]{1,0:T(1,128)}, u32[]{:S(2)}) copy-start(f32[1,24]{1,0:T(1,128)} %param.13) | copy-start | bytes 292
Sparse Core Ops, SparseCore 0:
  34.2 94.4 all-gather.1
  532.4 23.4 reduce-scatter.1
where the time goes:
time: 566 us; the launch traced here: 564 us
  other arithmetic  303 us (54%)
  waiting for transfers between devices  102 us (18%)
  local copies, waits for them, and re-layouts  88.4 us (16%)
  starting transfers between devices  30.2 us (5%)
  matrix products  24.8 us (4%)
  between operations  13.6 us (2%)
    another operation x48, other arithmetic  292 us
    gather x16, local copies, waits for them, and re-layouts, image_blocks(): screen_table[station_one].astype(jnp.float32)  35 us
    gather x16, local copies, waits for them, and re-layouts, image_blocks(): screen_table[station_two].astype(jnp.float32)  35 us
    all_gather x1, waiting for transfers between devices, shards(): screen_table = lax.all_gather(screens, 'grid', axis=0, tiled=True)  32.8 us
    all_to_all x1, waiting for transfers between devices, shards(): lax.all_to_all(payload.reshape((grid_count, capacity) + payload.shape[1:]...  24.7 us
    reduce_scatter x1, waiting for transfers between devices, shards(): lax.psum_scatter(leading_term + jnp.einsum('ar,prw->apw', sine_rows, exch...  23.6 us
    dot_general x16, matrix products, image_blocks(): jnp.einsum('gxk,gky->gxy', left_rows, right_cols, preferred_element_type=...  18.2 us
    all_to_all x1, starting transfers between devices, shards(): lax.all_to_all(block_tags.reshape(grid_count, capacity, 3), 'grid', split...  17.4 us
  transfers between devices with their start and end apart: 5, of which 5 were waited for; matrix products, arithmetic and copies ran while one was open for 1% of the time, Pallas kernels for 0%

commit v1 on v0

v1 whole, which is shorter than its diff:
```python
import math

import jax
import jax.numpy as jnp
import numpy as np
from jax import lax
from jax.experimental import pallas as pl
from jax.experimental.pallas import tpu as pltpu
from jax.sharding import PartitionSpec as P

SUB = 64
TS = 16
CH = 24
VIS = TS * CH
SG_DEV = 8
CAP = 2
LANES = 128
CHUNKS = VIS // LANES
SLOT_ROWS = 8
HALF_ROWS = SUB * SUB // 2 // LANES
MSG_ROWS = CAP * SLOT_ROWS + HALF_ROWS

ACROSS = np.array([a + s * (b + 0.5) for a in (-24, -8, 8, 24) for s in (1, -1) for b in range(8)])
DOWN_HALF = np.array([a + s * (b + 0.5) for a in (8, 24) for s in (1, -1) for b in range(8)])
DOWN = np.concatenate([DOWN_HALF, -DOWN_HALF])
PERM_X = (ACROSS + 31.5).astype(np.int64)
PERM_Y = (DOWN + 31.5).astype(np.int64)


def taper_and_dft():
    taper = np.sin(math.pi * (np.arange(SUB) + 0.5) / SUB)
    window = taper[PERM_Y][:, None] * taper[PERM_X][None, :] / VIS
    window = np.concatenate([window, window], axis=1)
    dft = np.exp(-2j * math.pi * np.outer(np.arange(SUB), np.arange(SUB)) / SUB) / math.sqrt(SUB)

    def real_form(perm):
        part = dft[:, perm].T
        return np.block([[part.real, part.imag], [-part.imag, part.real]])

    return (
        window.astype(np.float32),
        real_form(PERM_X).astype(np.float32),
        real_form(PERM_Y).astype(np.float32),
    )


def coordinate_spread():
    spread = np.zeros((LANES, 2 * VIS), np.float32)
    for axis in range(2):
        for piece in range(3):
            for t in range(TS):
                spread[(axis * 3 + piece) * TS + t, axis * VIS + t * CH : axis * VIS + (t + 1) * CH] = 1.0
    return spread


def sincos(angle):
    square = angle * angle
    sine = angle * (
        1.0
        + square
        * (
            -1.0 / 6
            + square * (1.0 / 120 + square * (-1.0 / 5040 + square * (1.0 / 362880)))
        )
    )
    cosine = 1.0 + square * (
        -0.5
        + square
        * (1.0 / 24 + square * (-1.0 / 720 + square * (1.0 / 40320 + square * (-1.0 / 3628800))))
    )
    return cosine, sine


def doubled(cosine, sine):
    twice = cosine + cosine
    return twice * cosine - 1.0, twice * sine


def half_steps(cosine, sine, cos_full):
    twice = cos_full + cos_full
    cos_list = [cosine, cosine * (twice - 1.0)]
    sin_list = [sine, sine * (twice + 1.0)]
    for _ in range(6):
        cos_list.append(twice * cos_list[-1] - cos_list[-2])
        sin_list.append(twice * sin_list[-1] - sin_list[-2])
    return cos_list, sin_list


def grid_kernel(
    tags,
    recv,
    other,
    scale,
    spread,
    window,
    across_dft,
    down_dft,
    out,
    rows,
    angles,
    beams,
    anchors,
    steps,
    total,
):
    sources = recv.shape[0]
    core = lax.rem(lax.axis_index("grid"), 2)
    lane = lax.broadcasted_iota(jnp.int32, (8, LANES), 1)
    low = lane < SUB

    def unpack(i, carry):
        rows[pl.ds(pl.multiple_of(i * 16, 16), 16), :] = recv[i, 0:16, :].astype(jnp.float32)
        mine = recv[i, 16:32, :].astype(jnp.float32)
        theirs = other[i].astype(jnp.float32)
        for half in range(2):
            part = jnp.where(core == half, mine, theirs)
            turned = pltpu.roll(part, SUB, 1)
            for j in range(2):
                a = part[8 * j : 8 * j + 8]
                b = turned[8 * j : 8 * j + 8]
                beams[i, half * 32 + j * 8 : half * 32 + j * 8 + 8, :] = jnp.where(low, a, b)
                beams[i, half * 32 + 16 + j * 8 : half * 32 + 16 + j * 8 + 8, :] = jnp.where(low, b, a)
        return carry

    lax.fori_loop(0, sources, unpack, 0, unroll=4)
    slots = sources * CAP
    coords = rows[pl.ds(6, slots, stride=SLOT_ROWS), :].astype(jnp.bfloat16)
    angles[...] = jnp.dot(coords, spread[...], preferred_element_type=jnp.float32) * scale[...]
    total[...] = jnp.zeros_like(total)
    sign = jnp.where(lax.broadcasted_iota(jnp.int32, (32, LANES), 1) < SUB, -1.0, 1.0)

    def anchor_row(part, chunk):
        return part * CHUNKS + chunk

    def group(g, carry):
        for c in range(CHUNKS):
            real = rows[pl.ds(g * 64 + c, 8, stride=SLOT_ROWS), :]
            imag = rows[pl.ds(g * 64 + CHUNKS + c, 8, stride=SLOT_ROWS), :]
            at = pl.ds(pl.multiple_of(g * 8, 8), 8)
            cu, su = sincos(angles[at, c * LANES : (c + 1) * LANES])
            cv, sv = sincos(angles[at, VIS + c * LANES : VIS + (c + 1) * LANES])
            cc = cu * cv - su * sv
            ss = su * cv + cu * sv
            xr = real * cc + imag * ss
            xi = imag * cc - real * ss
            for axis, (cosine, sine) in enumerate(((cu, su), (cv, sv))):
                c1, s1 = doubled(cosine, sine)
                cos_list, sin_list = half_steps(cosine, sine, c1)
                for b in range(8):
                    for part, value in ((2 * axis, cos_list[b]), (2 * axis + 1, sin_list[b])):
                        steps[pl.ds((part * CHUNKS + c) * 8 + b, 8, stride=4 * CHUNKS * 8), :] = value
                c8, s8 = doubled(*doubled(*doubled(c1, s1)))
                c16, s16 = doubled(c8, s8)
                twice = c8 + c8
                c24, s24 = twice * c16 - c8, twice * s16 - s8
                if axis == 0:
                    values = []
                    for ca, sa in ((c24, s24), (c8, s8)):
                        p, q, r, t = xr * ca, xi * sa, xr * sa, xi * ca
                        values.append(((p + q, t - r), (p - q, t + r)))
                    ordered = (values[0][0], values[1][0], values[1][1], values[0][1])
                    for a in range(4):
                        for k in range(2):
                            anchors[anchor_row(2 * a + k, c)] = ordered[a][k]
                else:
                    for a, pair in enumerate(((c8, s8), (c24, s24))):
                        for k in range(2):
                            anchors[anchor_row(8 + 2 * a + k, c)] = pair[k]
        for s in range(8):

            def step(part, c):
                first = ((s * 4 + part) * CHUNKS + c) * 8
                return steps[first : first + 8, :]

            def anchor(part, c):
                return jnp.broadcast_to(anchors[anchor_row(part, c), s : s + 1, :], (8, LANES))

            left = [[None] * CHUNKS for _ in range(8)]
            right = [[None] * CHUNKS for _ in range(4)]
            for c in range(CHUNKS):
                d, e = step(0, c), step(1, c)
                for a in range(4):
                    pr, pi = anchor(2 * a, c), anchor(2 * a + 1, c)
                    rd, ie, re, id_ = pr * d, pi * e, pr * e, pi * d
                    left[a][c] = jnp.concatenate([rd - ie, rd + ie], axis=0).astype(jnp.bfloat16)
                    left[4 + a][c] = jnp.concatenate([id_ + re, id_ - re], axis=0).astype(jnp.bfloat16)
                d, e = step(2, c), step(3, c)
                for a in range(2):
                    ca, sa = anchor(8 + 2 * a, c), anchor(9 + 2 * a, c)
                    cd, se, sd, ce = ca * d, sa * e, sa * d, ca * e
                    right[a][c] = jnp.concatenate([cd - se, cd + se], axis=0).astype(jnp.bfloat16)
                    right[2 + a][c] = jnp.concatenate([sd + ce, sd - ce], axis=0).astype(jnp.bfloat16)
            left_all = jnp.concatenate([jnp.concatenate(r, axis=1) for r in left], axis=0)
            right_all = jnp.concatenate([jnp.concatenate(r, axis=1) for r in right], axis=0)
            product = lax.dot_general(
                right_all, left_all, (((1,), (1,)), ((), ())), preferred_element_type=jnp.float32
            )
            top = product[:32]
            turned = pltpu.roll(product[32:], SUB, 1) * sign
            image = jnp.concatenate([top + turned, top - turned], axis=0)
            slot = g * 8 + s
            target = tags[3 * slot]
            gain = beams[tags[3 * slot + 1]] * beams[tags[3 * slot + 2]]
            total[target] += gain * image
        return carry

    lax.fori_loop(0, slots // 8, group, 0)
    exact = lax.Precision.HIGHEST
    for g in range(SG_DEV):
        tapered = total[g] * window[...]
        first = jnp.dot(tapered, across_dft[...], precision=exact, preferred_element_type=jnp.float32)
        stacked = jnp.concatenate([first[:, :SUB], first[:, SUB:]], axis=0)
        second = lax.dot_general(
            stacked,
            down_dft[...],
            (((0,), (0,)), ((), ())),
            precision=exact,
            preferred_element_type=jnp.float32,
        )
        bands = out.shape[0]
        each = SUB // bands
        for b in range(bands):
            out[b, g] = second[b * each : (b + 1) * each]


def packed_blocks(visibility, weights, block_uv, targets, stations, grid_count):
    blocks = visibility.shape[0]
    owner = targets // SG_DEV
    order = jnp.arange(blocks, dtype=jnp.int32)
    earlier = (owner[:, None] == owner[None, :]) & (order[:, None] < order[None, :])
    rank = jnp.sum(earlier.astype(jnp.int32), axis=0)
    position = owner * CAP + rank
    choose = (jnp.arange(grid_count * CAP, dtype=jnp.int32)[:, None] == position[None, :]).astype(
        jnp.bfloat16
    )
    weighted = (visibility * weights[:, None, :]).reshape(blocks, 2 * VIS).astype(jnp.bfloat16)
    high = lax.reduce_precision(block_uv, 8, 7)
    rest = block_uv - high
    middle = lax.reduce_precision(rest, 8, 7)
    pieces = jnp.stack([high, middle, rest - middle], axis=2).reshape(blocks, 2 * 3 * TS)
    numbers = jnp.concatenate([(targets % SG_DEV)[:, None], stations], axis=1).astype(jnp.float32)
    line = jnp.concatenate([pieces, numbers], axis=1).astype(jnp.bfloat16)
    line = jnp.concatenate(
        [weighted, line, jnp.zeros((blocks, SLOT_ROWS * LANES - 2 * VIS - line.shape[1]), jnp.bfloat16)],
        axis=1,
    )
    placed = jnp.dot(choose, line, preferred_element_type=jnp.float32).astype(jnp.bfloat16)
    return placed.reshape(grid_count, CAP * SLOT_ROWS, LANES)


def screen_halves(screen):
    turn_y = np.zeros((SUB, SUB), np.float32)
    turn_y[np.arange(SUB), PERM_Y] = 1.0
    turn_x = np.zeros((SUB, SUB), np.float32)
    turn_x[np.arange(SUB), PERM_X] = 1.0
    turned = jnp.dot(turn_y.astype(jnp.bfloat16), screen.T, preferred_element_type=jnp.float32)
    turned = jnp.dot(
        turned.astype(jnp.bfloat16), turn_x.T.astype(jnp.bfloat16), preferred_element_type=jnp.float32
    ).astype(jnp.bfloat16)
    halves = turned.reshape(2, 2, HALF_ROWS, SUB)
    return jnp.concatenate([halves[:, 0], halves[:, 1]], axis=2)


def gridded(tags, recv, other, scale, bands):
    slots = recv.shape[0] * CAP
    window, across_dft, down_dft = taper_and_dft()
    vmem = pl.BlockSpec(memory_space=pltpu.VMEM)
    return pl.pallas_call(
        grid_kernel,
        out_shape=jax.ShapeDtypeStruct((bands, SG_DEV, SUB // bands, LANES), jnp.float32),
        in_specs=[pl.BlockSpec(memory_space=pltpu.SMEM)] + [vmem] * 7,
        out_specs=vmem,
        scratch_shapes=[
            pltpu.VMEM((slots * SLOT_ROWS, LANES), jnp.float32),
            pltpu.VMEM((slots, 2 * VIS), jnp.float32),
            pltpu.VMEM((recv.shape[0], SUB, LANES), jnp.float32),
            pltpu.VMEM((12 * CHUNKS, 8, LANES), jnp.float32),
            pltpu.VMEM((8 * 4 * CHUNKS * 8, LANES), jnp.float32),
            pltpu.VMEM((SG_DEV, SUB, LANES), jnp.float32),
        ],
        compiler_params=pltpu.CompilerParams(vmem_limit_bytes=40 * 1024 * 1024),
        name="grid_blocks",
    )(
        tags,
        recv,
        other,
        scale,
        jnp.asarray(coordinate_spread(), jnp.bfloat16),
        jnp.asarray(window),
        jnp.asarray(across_dft),
        jnp.asarray(down_dft),
    )


def shards(visibility, weights, block_uv, chan_ratio, block_subgrid, block_stations, screens):
    grid_count = lax.axis_size("grid")
    bands = lax.axis_size("band")
    placed = packed_blocks(
        visibility[0], weights[0], block_uv, block_subgrid[0], block_stations, grid_count
    )
    halves = screen_halves(screens[0])
    sent_halves = jnp.broadcast_to(halves[None], (grid_count // 2,) + halves.shape).reshape(
        grid_count, HALF_ROWS, LANES
    )
    message = jnp.concatenate([placed, sent_halves], axis=1)
    recv = lax.all_to_all(message, "grid", split_axis=0, concat_axis=0, tiled=True)
    other = lax.ppermute(
        recv[:, CAP * SLOT_ROWS :], "grid", [(i, i ^ 1) for i in range(grid_count)]
    )
    first = 2 * 3 * TS
    tags = recv[:, : CAP * SLOT_ROWS].reshape(grid_count * CAP, SLOT_ROWS, LANES)[
        :, 2 * CHUNKS, first : first + 3
    ]
    tags = tags.astype(jnp.int32).reshape(-1)
    scale = jnp.tile(chan_ratio[0] * (math.pi / SUB), 2 * TS)[None, :]
    rows = gridded(tags, recv, other, scale, bands)
    parts = lax.all_to_all(rows, "band", split_axis=0, concat_axis=0, tiled=True)
    return jnp.transpose(jnp.sum(parts, axis=0), (1, 0, 2))


def solution(mesh):
    in_specs = (
        P("band", "grid", None, None),
        P("band", "grid", None),
        P("grid", None, None),
        P("band", None),
        P("band", "grid"),
        P("grid", None),
        P("grid", None, None),
    )
    out_specs = P("band", "grid", None)
    return jax.shard_map(shards, mesh=mesh, in_specs=in_specs, out_specs=out_specs, check_vma=False)
```

time: 566 us -> 102 us (0.18)
  other arithmetic: 303 us -> 3.81 us
  waiting for transfers between devices: 102 us -> 1.27 us
  local copies, waits for them, and re-layouts: 88.4 us -> 3.25 us
  blocking collectives: 0 us -> 59.7 us
  Pallas kernels: 0 us -> 30 us
  starting transfers between devices: 30.2 us -> 1.92 us
  matrix products: 24.8 us -> 1.29 us
  between operations: 13.6 us -> 0.2 us
    another operation x49 -> x4, other arithmetic: 292 us -> 1.43 us  [the longest x2 0.73 us: packed_blocks(): jnp.stack([high, middle, rest - middle], axis=2).reshape(blocks, 2 * 3 * TS)]
    gather x36 -> x0, local copies, waits for them, and re-layouts: 73.3 us -> none  [the longest x16 35 us: image_blocks(): screen_table[station_one].astype(jnp.float32)]
    all_to_all x0 -> x2, blocking collectives: none -> 59.7 us  [the longest x1 48.6 us: shards(): lax.all_to_all(message, 'grid', split_axis=0, concat_axis=0, tiled=True)]
    all_to_all x3 -> x0, waiting for transfers between devices: 44.9 us -> none  [the longest x1 24.7 us: shards(): lax.all_to_all(payload.reshape((grid_count, capacity) + payload.shape[1:]...]
    all_gather x1 -> x0, waiting for transfers between devices: 32.8 us -> none  [shards(): screen_table = lax.all_gather(screens, 'grid', axis=0, tiled=True)]
    all_to_all x3 -> x0, starting transfers between devices: 30 us -> none  [the longest x1 17.4 us: shards(): lax.all_to_all(block_tags.reshape(grid_count, capacity, 3), 'grid', split...]
    pallas_call x0 -> x1, Pallas kernels: none -> 30 us  [gridded(): pl.pallas_call(grid_kernel, out_shape=jax.ShapeDtypeStruct((bands, SG_DEV...]
    reduce_scatter x1 -> x0, waiting for transfers between devices: 23.6 us -> none  [shards(): lax.psum_scatter(leading_term + jnp.einsum('ar,prw->apw', sine_rows, exch...]
  transfers between devices with their start and end apart: 5 -> 1, of which waited for: 5 -> 1; matrix products, arithmetic and copies ran while one was open for 1% -> 1% of each run, Pallas kernels for 0% -> 0%
where the time goes in v1:
time: 102 us; the launch traced here: 101 us
  blocking collectives  59.7 us (59%)
  Pallas kernels  30 us (29%)
  other arithmetic  3.81 us (4%)
  local copies, waits for them, and re-layouts  3.25 us (3%)
  starting transfers between devices  1.92 us (2%)
  matrix products  1.29 us (1%)
  waiting for transfers between devices  1.27 us (1%)
    all_to_all x1, blocking collectives, shards(): lax.all_to_all(message, 'grid', split_axis=0, concat_axis=0, tiled=True)  48.6 us
    pallas_call x1, Pallas kernels, gridded(): pl.pallas_call(grid_kernel, out_shape=jax.ShapeDtypeStruct((bands, SG_DEV...  30 us
    all_to_all x1, blocking collectives, shards(): lax.all_to_all(rows, 'band', split_axis=0, concat_axis=0, tiled=True)  11.1 us
  transfers between devices with their start and end apart: 1, of which 1 were waited for; matrix products, arithmetic and copies ran while one was open for 1% of the time, Pallas kernels for 0%

profile of v1, /device:TPU:8, one launch (start us, length us, event | category | flops | bytes accessed | tf_op | source)
XLA Modules:
  0.0 101.4 jit_solution(7924304463988355083)
XLA Ops:
  0.0 0.7 and_select_fusion
  0.7 0.7 fusion.22
  1.4 0.7 and_select_fusion.1
  2.0 1.0 convolution_convert_fusion.1
  3.0 0.7 fusion.15
  3.7 0.1 copy.32
  3.9 0.7 fusion.13
  4.6 0.1 copy.31
  4.7 1.0 %copy.38 = f32[16,8,2,384]{3,1,2,0:T(8,128)S(1)} copy(f32[16,8,2,384]{3,2,1,0:T(2,128)} %bitcast.60) | data formatting | bytes 786432
  5.8 0.1 mul.27
  6.0 0.1 convert_reduce_fusion
  6.2 0.3 convolution_convert_fusion
  6.5 0.2 reshape.107
  6.8 0.1 pad_maximum_fusion.2
  7.0 48.6 %all_to_all.10.recv = bf16[128,32,128]{2,1,0:T(8,128)(2,1)S(1)} all-to-all(bf16[128,32,128]{2,1,0:T(8,128)(2,1)S(1)} %pad_maximum_fusion), channel_id=1, replica_groups=mesh['grid'=128,'band'=4] {'grid'}, dimensions={0} | all-to-all | bytes 2097152 | tf_op jit(solution)/shard_map/all_to_all | solution.py:306
  55.7 0.2 fusion.19
  55.9 1.9 %collective-permute-start = (bf16[128,16,128]{2,1,0:T(8,128)(2,1)S(1)}, bf16[128,16,128]{2,1,0:T(8,128)(2,1)S(1)}, u32[]{:S(2)}, u32[]{:S(2)}) collective-permute-start(bf16[128,16,128]{2,1,0:T(8,128)(2,1)S(1)} %get-tuple-element.5), channel_id=1, source_target_pairs={{0,4},{4,0},{8,12},{12,8},{16,20},{20,16},{24,28},{28,24},{32,36},... | collective-permute-start | bytes 1572872 | tf_op jit(solution)/shard_map/ppermute | solution.py:307
  57.8 0.1 broadcast_in_dim_tile.3.scale
  57.9 0.3 slice.23
  58.2 0.2 reshape.111.tags
  58.4 1.3 %collective-permute-done.other = bf16[128,16,128]{2,1,0:T(8,128)(2,1)S(1)} collective-permute-done((bf16[128,16,128]{2,1,0:T(8,128)(2,1)S(1)}, bf16[128,16,128]{2,1,0:T(8,128)(2,1)S(1)}, u32[]{:S(2)}, u32[]{:S(2)}) %collective-permute-start) | collective-permute-done | bytes 524320 | tf_op jit(solution)/shard_map/ppermute | solution.py:307
  59.7 30.0 %grid_blocks.1 = f32[4,8,16,128]{3,2,1,0:T(8,128)S(1)} custom-call(s32[768]{0:T(1024)S(1)} %reshape.111.tags, bf16[128,32,128]{2,1,0:T(8,128)(2,1)S(1)} %all_to_all.10.recv, bf16[128,16,128]{2,1,0:T(8,128)(2,1)S(1)} %collective-permute-done.other, f32[1,768]{1,0:T(1,128)S(1)} %broadcast_in_dim_tile.3.scale, bf16[128,768]{1,0:T(8,128)(2,1)S(1)} %copy-done.1, ...), custom_call_target="tpu_custom_call" | custom-call | tf_op jit(solution)/shard_map/grid_blocks/pallas_call | solution.py:268
  89.6 11.1 %all_to_all.11 = f32[4,8,16,128]{3,2,1,0:T(8,128)S(1)} all-to-all(f32[4,8,16,128]{3,2,1,0:T(8,128)S(1)} %grid_blocks.1), channel_id=1, replica_groups=mesh['grid'=128,'band'=4] {'band'}, dimensions={0} | all-to-all | bytes 524288 | tf_op jit(solution)/shard_map/all_to_all | solution.py:317
  100.7 0.7 copy.35
  (29 shorter events, 0.4 us)
Async XLA Ops:
  0.0 2.0 %copy-start = (bf16[1,64,64]{2,1,0:T(8,128)(2,1)S(1)}, bf16[1,64,64]{2,1,0:T(8,128)(2,1)}, u32[]{:S(2)}) copy-start(bf16[1,64,64]{2,1,0:T(8,128)(2,1)} %param.19) | copy-start | bytes 24580
  0.0 5.8 %copy-start.5 = (f32[1,128,384]{2,1,0:T(8,128)S(1)}, f32[1,128,384]{2,1,0:T(8,128)}, u32[]{:S(2)}) copy-start(f32[1,128,384]{2,1,0:T(8,128)} %param.14) | copy-start | bytes 589828
  4.7 1.3 %copy-start.6 = (s32[1,128]{1,0:T(1,128)S(1)}, s32[1,128]{1,0:T(1,128)}, u32[]{:S(2)}) copy-start(s32[1,128]{1,0:T(1,128)} %param.17) | copy-start | bytes 1540
  55.6 2.1 %copy-start.7 = (f32[1,24]{1,0:T(1,128)S(1)}, f32[1,24]{1,0:T(1,128)}, u32[]{:S(2)}) copy-start(f32[1,24]{1,0:T(1,128)} %param.16) | copy-start | bytes 292
  55.6 4.0 %copy-start.1 = (bf16[128,768]{1,0:T(8,128)(2,1)S(1)}, bf16[128,768]{1,0:T(8,128)(2,1)}, u32[]{:S(2)}) copy-start(bf16[128,768]{1,0:T(8,128)(2,1)} %constant.51.clone.spread) | copy-start | bytes 589828
  55.6 4.0 %copy-start.2 = (f32[128,128]{1,0:T(8,128)S(1)}, f32[128,128]{1,0:T(8,128)}, u32[]{:S(2)}) copy-start(f32[128,128]{1,0:T(8,128)} %constant.53.clone.across_dft) | copy-start | bytes 196612
  55.6 4.0 %copy-start.3 = (f32[128,128]{1,0:T(8,128)S(1)}, f32[128,128]{1,0:T(8,128)}, u32[]{:S(2)}) copy-start(f32[128,128]{1,0:T(8,128)} %constant.54.clone.down_dft) | copy-start | bytes 196612
  55.7 4.0 %copy-start.4 = (f32[64,128]{1,0:T(8,128)S(1)}, f32[64,128]{1,0:T(8,128)}, u32[]{:S(2)}) copy-start(f32[64,128]{1,0:T(8,128)} %constant.52.clone.window) | copy-start | bytes 98308
  55.9 3.8 %collective-permute-start = (bf16[128,16,128]{2,1,0:T(8,128)(2,1)S(1)}, bf16[128,16,128]{2,1,0:T(8,128)(2,1)S(1)}, u32[]{:S(2)}, u32[]{:S(2)}) collective-permute-start(bf16[128,16,128]{2,1,0:T(8,128)(2,1)S(1)} %get-tuple-element.5), channel_id=1, source_target_pairs={{0,4},{4,0},{8,12},{12,8},{16,20},{20,16},{24,28},{28,24},{32,36},... | collective-permute-start | bytes 1572872 | tf_op jit(solution)/shard_map/ppermute | solution.py:307

commit v2 on v1

--- a/solution.py
+++ b/solution.py
@@ -16,9 +16,11 @@
 CAP = 2
 LANES = 128
 CHUNKS = VIS // LANES
+GROUPS_A_TURN = 8
 SLOT_ROWS = 8
 HALF_ROWS = SUB * SUB // 2 // LANES
 MSG_ROWS = CAP * SLOT_ROWS + HALF_ROWS
+PITCH = 264
 
 ACROSS = np.array([a + s * (b + 0.5) for a in (-24, -8, 8, 24) for s in (1, -1) for b in range(8)])
 DOWN_HALF = np.array([a + s * (b + 0.5) for a in (8, 24) for s in (1, -1) for b in range(8)])
@@ -49,7 +51,7 @@
     for axis in range(2):
         for piece in range(3):
             for t in range(TS):
-                spread[(axis * 3 + piece) * TS + t, axis * VIS + t * CH : axis * VIS + (t + 1) * CH] = 1.0
+                spread[(piece * 2 + axis) * TS + t, axis * VIS + t * CH : axis * VIS + (t + 1) * CH] = 1.0
     return spread
 
 
@@ -99,9 +101,8 @@
     rows,
     angles,
     beams,
-    anchors,
-    steps,
     total,
+    *buffers,
 ):
     sources = recv.shape[0]
     core = lax.rem(lax.axis_index("grid"), 2)
@@ -122,7 +123,7 @@
                 beams[i, half * 32 + 16 + j * 8 : half * 32 + 16 + j * 8 + 8, :] = jnp.where(low, b, a)
         return carry
 
-    lax.fori_loop(0, sources, unpack, 0, unroll=4)
+    lax.fori_loop(0, sources, unpack, 0, unroll=16)
     slots = sources * CAP
     coords = rows[pl.ds(6, slots, stride=SLOT_ROWS), :].astype(jnp.bfloat16)
     angles[...] = jnp.dot(coords, spread[...], preferred_element_type=jnp.float32) * scale[...]
@@ -132,7 +133,7 @@
     def anchor_row(part, chunk):
         return part * CHUNKS + chunk
 
-    def group(g, carry):
+    def base(g, anchors, steps):
         for c in range(CHUNKS):
             real = rows[pl.ds(g * 64 + c, 8, stride=SLOT_ROWS), :]
             imag = rows[pl.ds(g * 64 + CHUNKS + c, 8, stride=SLOT_ROWS), :]
@@ -148,7 +149,8 @@
                 cos_list, sin_list = half_steps(cosine, sine, c1)
                 for b in range(8):
                     for part, value in ((2 * axis, cos_list[b]), (2 * axis + 1, sin_list[b])):
-                        steps[pl.ds((part * CHUNKS + c) * 8 + b, 8, stride=4 * CHUNKS * 8), :] = value
+                        first = (part * CHUNKS + c) * 64 + b * 8
+                        steps[first : first + 8, :] = value
                 c8, s8 = doubled(*doubled(*doubled(c1, s1)))
                 c16, s16 = doubled(c8, s8)
                 twice = c8 + c8
@@ -166,11 +168,12 @@
                     for a, pair in enumerate(((c8, s8), (c24, s24))):
                         for k in range(2):
                             anchors[anchor_row(8 + 2 * a + k, c)] = pair[k]
+
+    def expand(g, anchors, steps):
         for s in range(8):
 
             def step(part, c):
-                first = ((s * 4 + part) * CHUNKS + c) * 8
-                return steps[first : first + 8, :]
+                return steps[pl.ds((part * CHUNKS + c) * 64 + s, 8, stride=8), :]
 
             def anchor(part, c):
                 return jnp.broadcast_to(anchors[anchor_row(part, c), s : s + 1, :], (8, LANES))
@@ -188,23 +191,33 @@
                 for a in range(2):
                     ca, sa = anchor(8 + 2 * a, c), anchor(9 + 2 * a, c)
                     cd, se, sd, ce = ca * d, sa * e, sa * d, ca * e
-                    right[a][c] = jnp.concatenate([cd - se, cd + se], axis=0).astype(jnp.bfloat16)
-                    right[2 + a][c] = jnp.concatenate([sd + ce, sd - ce], axis=0).astype(jnp.bfloat16)
+                    right[a][c] = jnp.concatenate([cd, se], axis=0).astype(jnp.bfloat16)
+                    right[2 + a][c] = jnp.concatenate([sd, ce], axis=0).astype(jnp.bfloat16)
             left_all = jnp.concatenate([jnp.concatenate(r, axis=1) for r in left], axis=0)
             right_all = jnp.concatenate([jnp.concatenate(r, axis=1) for r in right], axis=0)
             product = lax.dot_general(
                 right_all, left_all, (((1,), (1,)), ((), ())), preferred_element_type=jnp.float32
             )
-            top = product[:32]
-            turned = pltpu.roll(product[32:], SUB, 1) * sign
+            q = [product[8 * j : 8 * j + 8] for j in range(8)]
+            top = jnp.concatenate([q[0] - q[1], q[0] + q[1], q[2] - q[3], q[2] + q[3]], axis=0)
+            bottom = jnp.concatenate([q[4] + q[5], q[4] - q[5], q[6] + q[7], q[6] - q[7]], axis=0)
+            turned = pltpu.roll(bottom, SUB, 1) * sign
             image = jnp.concatenate([top + turned, top - turned], axis=0)
             slot = g * 8 + s
             target = tags[3 * slot]
             gain = beams[tags[3 * slot + 1]] * beams[tags[3 * slot + 2]]
             total[target] += gain * image
+
+    turns = slots // 8 // GROUPS_A_TURN
+
+    def turn(i, carry):
+        for j in range(GROUPS_A_TURN):
+            at = 2 * (j % 2)
+            base(GROUPS_A_TURN * i + j, *buffers[at : at + 2])
+            expand(GROUPS_A_TURN * i + j, *buffers[at : at + 2])
         return carry
 
-    lax.fori_loop(0, slots // 8, group, 0)
+    lax.fori_loop(0, turns, turn, 0)
     exact = lax.Precision.HIGHEST
     for g in range(SG_DEV):
         tapered = total[g] * window[...]
@@ -223,42 +236,99 @@
             out[b, g] = second[b * each : (b + 1) * each]
 
 
-def packed_blocks(visibility, weights, block_uv, targets, stations, grid_count):
+def pack_kernel(visibility, weights, coords, owned, stations, screen, turn_y, turn_x, out, placed):
+    blocks = weights.shape[0]
+    dests = out.shape[0]
+    lined = jnp.broadcast_to((owned[...] // SG_DEV).astype(jnp.float32), (blocks, blocks))
+    first = lax.broadcasted_iota(jnp.int32, (blocks, blocks), 0)
+    second = lax.broadcasted_iota(jnp.int32, (blocks, blocks), 1)
+    earlier = jnp.where((lined.T == lined) & (first < second), 1.0, 0.0)
+    rank = jnp.sum(earlier, axis=0, keepdims=True)
+    dest = lax.broadcasted_iota(jnp.int32, (dests, blocks), 0).astype(jnp.float32)
+    here = jnp.broadcast_to(lined[:1], (dests, blocks)) == dest
+    ranks = jnp.broadcast_to(rank, (dests, blocks))
+    choose = jnp.concatenate(
+        [jnp.where(here & (ranks == k), 1.0, 0.0) for k in range(CAP)], axis=0
+    ).astype(jnp.bfloat16)
+    for c in range(CHUNKS):
+        weight = weights[:, c * LANES : (c + 1) * LANES]
+        for k in range(2):
+            weighted = visibility[:, k, c * LANES : (c + 1) * LANES] * weight
+            at = (k * CHUNKS + c) * PITCH
+            placed[at : at + CAP * dests, :] = jnp.dot(
+                choose, weighted.astype(jnp.bfloat16), preferred_element_type=jnp.float32
+            )
+    rest = coords[...]
+    pieces = []
+    for _ in range(3):
+        pieces.append(rest.astype(jnp.bfloat16).astype(jnp.float32))
+        rest = rest - pieces[-1]
+    local = (owned[...] % SG_DEV).astype(jnp.float32)
+    numbers = jnp.concatenate(
+        [local, stations[...].astype(jnp.float32), jnp.zeros((5, blocks), jnp.float32)], axis=0
+    )
+    empty = jnp.zeros((LANES - 3 * coords.shape[0] - 8, blocks), jnp.float32)
+    line = jnp.concatenate(pieces + [numbers, empty], axis=0).astype(jnp.bfloat16)
+    at = 2 * CHUNKS * PITCH
+    placed[at : at + CAP * dests, :] = lax.dot_general(
+        choose, line, (((1,), (1,)), ((), ())), preferred_element_type=jnp.float32
+    )
+    at = (2 * CHUNKS + 1) * PITCH
+    placed[at : at + CAP * dests, :] = jnp.zeros((CAP * dests, LANES), jnp.float32)
+    turned = lax.dot_general(
+        turn_y[...], screen[...], (((1,), (1,)), ((), ())), preferred_element_type=jnp.float32
+    ).astype(jnp.bfloat16)
+    halves = []
+    for h in range(2):
+        sides = [
+            jnp.dot(
+                turned[32 * h + 16 * k : 32 * h + 16 * k + 16],
+                turn_x[k],
+                preferred_element_type=jnp.float32,
+            )
+            for k in range(2)
+        ]
+        halves.append((sides[0] + sides[1]).astype(jnp.bfloat16))
+
+    def write(i, carry):
+        for h in range(2):
+            d = 2 * i + h
+            rows = [
+                placed[pl.ds(k * dests + d, SLOT_ROWS, stride=PITCH), :] for k in range(CAP)
+            ]
+            out[d, 0 : CAP * SLOT_ROWS, :] = jnp.concatenate(rows, axis=0).astype(jnp.bfloat16)
+            out[d, CAP * SLOT_ROWS :, :] = halves[h]
+        return carry
+
+    lax.fori_loop(0, dests // 2, write, 0, unroll=8)
+
+
+def packed(visibility, weights, block_uv, targets, stations, screen, grid_count):
     blocks = visibility.shape[0]
-    owner = targets // SG_DEV
-    order = jnp.arange(blocks, dtype=jnp.int32)
-    earlier = (owner[:, None] == owner[None, :]) & (order[:, None] < order[None, :])
-    rank = jnp.sum(earlier.astype(jnp.int32), axis=0)
-    position = owner * CAP + rank
-    choose = (jnp.arange(grid_count * CAP, dtype=jnp.int32)[:, None] == position[None, :]).astype(
-        jnp.bfloat16
-    )
-    weighted = (visibility * weights[:, None, :]).reshape(blocks, 2 * VIS).astype(jnp.bfloat16)
-    high = lax.reduce_precision(block_uv, 8, 7)
-    rest = block_uv - high
-    middle = lax.reduce_precision(rest, 8, 7)
-    pieces = jnp.stack([high, middle, rest - middle], axis=2).reshape(blocks, 2 * 3 * TS)
-    numbers = jnp.concatenate([(targets % SG_DEV)[:, None], stations], axis=1).astype(jnp.float32)
-    line = jnp.concatenate([pieces, numbers], axis=1).astype(jnp.bfloat16)
-    line = jnp.concatenate(
-        [weighted, line, jnp.zeros((blocks, SLOT_ROWS * LANES - 2 * VIS - line.shape[1]), jnp.bfloat16)],
-        axis=1,
-    )
-    placed = jnp.dot(choose, line, preferred_element_type=jnp.float32).astype(jnp.bfloat16)
-    return placed.reshape(grid_count, CAP * SLOT_ROWS, LANES)
-
-
-def screen_halves(screen):
     turn_y = np.zeros((SUB, SUB), np.float32)
     turn_y[np.arange(SUB), PERM_Y] = 1.0
-    turn_x = np.zeros((SUB, SUB), np.float32)
-    turn_x[np.arange(SUB), PERM_X] = 1.0
-    turned = jnp.dot(turn_y.astype(jnp.bfloat16), screen.T, preferred_element_type=jnp.float32)
-    turned = jnp.dot(
-        turned.astype(jnp.bfloat16), turn_x.T.astype(jnp.bfloat16), preferred_element_type=jnp.float32
-    ).astype(jnp.bfloat16)
-    halves = turned.reshape(2, 2, HALF_ROWS, SUB)
-    return jnp.concatenate([halves[:, 0], halves[:, 1]], axis=2)
+    turn_x = np.zeros((2, SUB, LANES), np.float32)
+    for k in range(2):
+        turn_x[k, PERM_X, k * SUB + np.arange(SUB)] = 1.0
+    vmem = pl.BlockSpec(memory_space=pltpu.VMEM)
+    return pl.pallas_call(
+        pack_kernel,
+        out_shape=jax.ShapeDtypeStruct((grid_count, MSG_ROWS, LANES), jnp.bfloat16),
+        in_specs=[vmem] * 8,
+        out_specs=vmem,
+        scratch_shapes=[pltpu.VMEM((SLOT_ROWS * PITCH, LANES), jnp.float32)],
+        compiler_params=pltpu.CompilerParams(vmem_limit_bytes=40 * 1024 * 1024),
+        name="pack_blocks",
+    )(
+        visibility,
+        weights,
+        block_uv.transpose(1, 2, 0).reshape(2 * TS, blocks),
+        targets,
+        stations.T,
+        screen,
+        jnp.asarray(turn_y, jnp.bfloat16),
+        jnp.asarray(turn_x, jnp.bfloat16),
+    )
 
 
 def gridded(tags, recv, other, scale, bands):
@@ -274,9 +344,11 @@
             pltpu.VMEM((slots * SLOT_ROWS, LANES), jnp.float32),
             pltpu.VMEM((slots, 2 * VIS), jnp.float32),
             pltpu.VMEM((recv.shape[0], SUB, LANES), jnp.float32),
+            pltpu.VMEM((SG_DEV, SUB, LANES), jnp.float32),
             pltpu.VMEM((12 * CHUNKS, 8, LANES), jnp.float32),
-            pltpu.VMEM((8 * 4 * CHUNKS * 8, LANES), jnp.float32),
-            pltpu.VMEM((SG_DEV, SUB, LANES), jnp.float32),
+            pltpu.VMEM((4 * CHUNKS * 64, LANES), jnp.float32),
+            pltpu.VMEM((12 * CHUNKS, 8, LANES), jnp.float32),
+            pltpu.VMEM((4 * CHUNKS * 64, LANES), jnp.float32),
         ],
         compiler_params=pltpu.CompilerParams(vmem_limit_bytes=40 * 1024 * 1024),
         name="grid_blocks",
@@ -295,14 +367,9 @@
 def shards(visibility, weights, block_uv, chan_ratio, block_subgrid, block_stations, screens):
     grid_count = lax.axis_size("grid")
     bands = lax.axis_size("band")
-    placed = packed_blocks(
-        visibility[0], weights[0], block_uv, block_subgrid[0], block_stations, grid_count
-    )
-    halves = screen_halves(screens[0])
-    sent_halves = jnp.broadcast_to(halves[None], (grid_count // 2,) + halves.shape).reshape(
-        grid_count, HALF_ROWS, LANES
-    )
-    message = jnp.concatenate([placed, sent_halves], axis=1)
+    message = packed(
+        visibility[0], weights[0], block_uv, block_subgrid, block_stations, screens[0], grid_count
+    )
     recv = lax.all_to_all(message, "grid", split_axis=0, concat_axis=0, tiled=True)
     other = lax.ppermute(
         recv[:, CAP * SLOT_ROWS :], "grid", [(i, i ^ 1) for i in range(grid_count)]

time: 102 us -> 87.1 us (0.85)
  Pallas kernels: 30 us -> 17.4 us
  other arithmetic: 3.81 us -> 0.05 us
  local copies, waits for them, and re-layouts: 3.25 us -> 6.24 us
  matrix products: 1.29 us -> 0 us
    pallas_call x1, Pallas kernels: 30 us -> 16.5 us  [gridded(): pl.pallas_call(grid_kernel, out_shape=jax.ShapeDtypeStruct((bands, SG_DEV...]
    unnamed x18 -> x26, local copies, waits for them, and re-layouts: 1.1 us -> 4.86 us
    another operation x3 -> x0, other arithmetic: 1.43 us -> none  [the longest x2 0.73 us: packed_blocks(): jnp.stack([high, middle, rest - middle], axis=2).reshape(blocks, 2 * 3 * TS)]
    select_n x2 -> x0, other arithmetic: 1.37 us -> none  [the longest x1 0.7 us: packed_blocks(): targets % SG_DEV]
    dot_general x2 -> x0, matrix products: 1.29 us -> none  [the longest x1 0.98 us: screen_halves(): jnp.dot(turned.astype(jnp.bfloat16), turn_x.T.astype(jnp.bfloat16), prefe...]
where the time goes in v2:
time: 87.1 us; the launch traced here: 86.6 us
  blocking collectives  59.7 us (69%)
  Pallas kernels  17.4 us (20%)
  local copies, waits for them, and re-layouts  6.24 us (7%)
  starting transfers between devices  1.92 us (2%)
  waiting for transfers between devices  1.21 us (1%)
    all_to_all x1, blocking collectives, shards(): lax.all_to_all(message, 'grid', split_axis=0, concat_axis=0, tiled=True)  48.6 us
    pallas_call x1, Pallas kernels, gridded(): pl.pallas_call(grid_kernel, out_shape=jax.ShapeDtypeStruct((bands, SG_DEV...  16.5 us
    all_to_all x1, blocking collectives, shards(): lax.all_to_all(rows, 'band', split_axis=0, concat_axis=0, tiled=True)  11.1 us
    unnamed x26, local copies, waits for them, and re-layouts  4.86 us
    ppermute x1, starting transfers between devices, shards(): lax.ppermute(recv[:, CAP * SLOT_ROWS:], 'grid', [(i, i ^ 1) for i in rang...  1.92 us
  transfers between devices with their start and end apart: 1, of which 1 were waited for; matrix products, arithmetic and copies ran while one was open for 1% of the time, Pallas kernels for 0%

profile of v2, /device:TPU:8, one launch (start us, length us, event | category | flops | bytes accessed | tf_op | source)
XLA Modules:
  0.0 86.6 jit_solution(9623482391483408048)
XLA Ops:
  0.0 0.7 copy-done.9
  0.7 0.0 copy-done.10
  0.7 1.0 %copy-done = f32[1,128,2,384]{3,2,1,0:T(2,128)S(1)} copy-done((f32[1,128,2,384]{3,2,1,0:T(2,128)S(1)}, f32[1,128,2,384]{3,2,1,0:T(2,128)}, u32[]{:S(2)}) %copy-start) | copy-done | bytes 393240
  1.7 0.9 %copy-done.2 = f32[1,128,384]{2,1,0:T(8,128)S(1)} copy-done((f32[1,128,384]{2,1,0:T(8,128)S(1)}, f32[1,128,384]{2,1,0:T(8,128)}, u32[]{:S(2)}) %copy-start.2) | copy-done | bytes 196632
  2.7 0.8 copy-done.6
  3.4 0.7 copy-done.7
  4.1 0.7 copy-done.8
  4.8 0.9 %pack_blocks.1 = bf16[128,32,128]{2,1,0:T(8,128)(2,1)S(1)} custom-call(f32[128,2,384]{2,1,0:T(2,128)S(1)} %bitcast.13, f32[128,384]{1,0:T(8,128)S(1)} %bitcast.14, f32[32,128]{1,0:T(8,128)S(1)} %bitcast.15, s32[1,128]{1,0:T(1,128)S(1)} %copy-done.11, s32[2,128]{1,0:T(2,128)S(1)} %bitcast.17, bf16[64,64]{1,0:T(8,128)(2,1)S(1)} %bitcast.16, ...), custom_call_target="tpu_custom_call" | custom-call | tf_op jit(solution)/shard_map/pack_blocks/pallas_call | solution.py:314
  5.7 48.6 %all_to_all.10.recv = bf16[128,32,128]{2,1,0:T(8,128)(2,1)S(1)} all-to-all(bf16[128,32,128]{2,1,0:T(8,128)(2,1)S(1)} %pack_blocks.1), channel_id=1, replica_groups=mesh['grid'=128,'band'=4] {'grid'}, dimensions={0} | all-to-all | bytes 2097152 | tf_op jit(solution)/shard_map/all_to_all | solution.py:373
  54.4 0.2 fusion
  54.6 0.0 copy-start.12
  54.6 1.9 %collective-permute-start = (bf16[128,16,128]{2,1,0:T(8,128)(2,1)S(1)}, bf16[128,16,128]{2,1,0:T(8,128)(2,1)S(1)}, u32[]{:S(2)}, u32[]{:S(2)}) collective-permute-start(bf16[128,16,128]{2,1,0:T(8,128)(2,1)S(1)} %get-tuple-element.5), channel_id=1, source_target_pairs={{0,4},{4,0},{8,12},{12,8},{16,20},{20,16},{24,28},{28,24},{32,36},... | collective-permute-start | bytes 1572872 | tf_op jit(solution)/shard_map/ppermute | solution.py:374
  56.5 0.1 broadcast_in_dim_tile.3.scale
  56.6 0.3 slice.13
  56.9 0.0 copy-start.1
  56.9 0.0 copy-start.5
  56.9 0.0 copy-start.3
  56.9 0.0 copy-start.4
  57.0 0.2 reshape.12.tags
  57.2 1.2 %collective-permute-done.other = bf16[128,16,128]{2,1,0:T(8,128)(2,1)S(1)} collective-permute-done((bf16[128,16,128]{2,1,0:T(8,128)(2,1)S(1)}, bf16[128,16,128]{2,1,0:T(8,128)(2,1)S(1)}, u32[]{:S(2)}, u32[]{:S(2)}) %collective-permute-start) | collective-permute-done | bytes 524320 | tf_op jit(solution)/shard_map/ppermute | solution.py:374
  58.4 0.0 copy-done.1
  58.4 16.5 %grid_blocks.1 = f32[4,8,16,128]{3,2,1,0:T(8,128)S(1)} custom-call(s32[768]{0:T(1024)S(1)} %reshape.12.tags, bf16[128,32,128]{2,1,0:T(8,128)(2,1)S(1)} %all_to_all.10.recv, bf16[128,16,128]{2,1,0:T(8,128)(2,1)S(1)} %collective-permute-done.other, f32[1,768]{1,0:T(1,128)S(1)} %broadcast_in_dim_tile.3.scale, bf16[128,768]{1,0:T(8,128)(2,1)S(1)} %copy-done.1, ...), custom_call_target="tpu_custom_call" | custom-call | tf_op jit(solution)/shard_map/grid_blocks/pallas_call | solution.py:338
  74.9 11.1 %all_to_all.11 = f32[4,8,16,128]{3,2,1,0:T(8,128)S(1)} all-to-all(f32[4,8,16,128]{3,2,1,0:T(8,128)S(1)} %grid_blocks.1), channel_id=1, replica_groups=mesh['grid'=128,'band'=4] {'band'}, dimensions={0} | all-to-all | bytes 524288 | tf_op jit(solution)/shard_map/all_to_all | solution.py:384
  86.0 0.7 copy.16
  (17 shorter events, 0.1 us)
Async XLA Ops:
  0.0 0.7 copy-start.9
  0.0 0.7 copy-start.10
  0.0 0.7 copy-start.11
  0.7 1.0 %copy-start = (f32[1,128,2,384]{3,2,1,0:T(2,128)S(1)}, f32[1,128,2,384]{3,2,1,0:T(2,128)}, u32[]{:S(2)}) copy-start(f32[1,128,2,384]{3,2,1,0:T(2,128)} %param.13) | copy-start | bytes 1179652
  1.7 0.9 %copy-start.2 = (f32[1,128,384]{2,1,0:T(8,128)S(1)}, f32[1,128,384]{2,1,0:T(8,128)}, u32[]{:S(2)}) copy-start(f32[1,128,384]{2,1,0:T(8,128)} %param.14) | copy-start | bytes 589828
  2.6 0.8 copy-start.6
  3.4 0.7 copy-start.7
  4.1 0.7 copy-start.8
  54.6 1.9 %copy-start.12 = (f32[1,24]{1,0:T(1,128)S(1)}, f32[1,24]{1,0:T(1,128)}, u32[]{:S(2)}) copy-start(f32[1,24]{1,0:T(1,128)} %param.16) | copy-start | bytes 292
  54.6 3.8 %collective-permute-start = (bf16[128,16,128]{2,1,0:T(8,128)(2,1)S(1)}, bf16[128,16,128]{2,1,0:T(8,128)(2,1)S(1)}, u32[]{:S(2)}, u32[]{:S(2)}) collective-permute-start(bf16[128,16,128]{2,1,0:T(8,128)(2,1)S(1)} %get-tuple-element.5), channel_id=1, source_target_pairs={{0,4},{4,0},{8,12},{12,8},{16,20},{20,16},{24,28},{28,24},{32,36},... | collective-permute-start | bytes 1572872 | tf_op jit(solution)/shard_map/ppermute | solution.py:374
  56.9 1.5 %copy-start.1 = (bf16[128,768]{1,0:T(8,128)(2,1)S(1)}, bf16[128,768]{1,0:T(8,128)(2,1)}, u32[]{:S(2)}) copy-start(bf16[128,768]{1,0:T(8,128)(2,1)} %constant.18.clone.spread) | copy-start | bytes 589828
  56.9 1.5 %copy-start.5 = (f32[64,128]{1,0:T(8,128)S(1)}, f32[64,128]{1,0:T(8,128)}, u32[]{:S(2)}) copy-start(f32[64,128]{1,0:T(8,128)} %constant.19.clone.window) | copy-start | bytes 98308
  56.9 1.5 %copy-start.3 = (f32[128,128]{1,0:T(8,128)S(1)}, f32[128,128]{1,0:T(8,128)}, u32[]{:S(2)}) copy-start(f32[128,128]{1,0:T(8,128)} %constant.20.clone.across_dft) | copy-start | bytes 196612
  56.9 1.4 %copy-start.4 = (f32[128,128]{1,0:T(8,128)S(1)}, f32[128,128]{1,0:T(8,128)}, u32[]{:S(2)}) copy-start(f32[128,128]{1,0:T(8,128)} %constant.21.clone.down_dft) | copy-start | bytes 196612

commit v3 on v2

--- a/solution.py
+++ b/solution.py
@@ -219,10 +219,13 @@
 
     lax.fori_loop(0, turns, turn, 0)
     exact = lax.Precision.HIGHEST
+    tapered = (total[...] * window[...]).reshape(SG_DEV * SUB, LANES)
+    first = jnp.dot(tapered, across_dft[...], precision=exact, preferred_element_type=jnp.float32)
+    bands = out.shape[0]
+    each = SUB // bands
     for g in range(SG_DEV):
-        tapered = total[g] * window[...]
-        first = jnp.dot(tapered, across_dft[...], precision=exact, preferred_element_type=jnp.float32)
-        stacked = jnp.concatenate([first[:, :SUB], first[:, SUB:]], axis=0)
+        mine = first[g * SUB : (g + 1) * SUB]
+        stacked = jnp.concatenate([mine[:, :SUB], mine[:, SUB:]], axis=0)
         second = lax.dot_general(
             stacked,
             down_dft[...],
@@ -230,13 +233,18 @@
             precision=exact,
             preferred_element_type=jnp.float32,
         )
-        bands = out.shape[0]
-        each = SUB // bands
         for b in range(bands):
-            out[b, g] = second[b * each : (b + 1) * each]
-
-
-def pack_kernel(visibility, weights, coords, owned, stations, screen, turn_y, turn_x, out, placed):
+            out[b, :, g, :] = second[b * each : (b + 1) * each]
+
+
+def pack_kernel(*refs):
+    sources, out, placed, held, done = refs[:8], refs[8], refs[9], refs[10:18], refs[18]
+    copies = [pltpu.make_async_copy(sources[i], held[i], done.at[i]) for i in range(8)]
+    for copy in copies:
+        copy.start()
+    visibility, weights, coords, owned, stations, screen, turn_y, turn_x = held
+    for copy in copies[2:]:
+        copy.wait()
     blocks = weights.shape[0]
     dests = out.shape[0]
     lined = jnp.broadcast_to((owned[...] // SG_DEV).astype(jnp.float32), (blocks, blocks))
@@ -250,14 +258,6 @@
     choose = jnp.concatenate(
         [jnp.where(here & (ranks == k), 1.0, 0.0) for k in range(CAP)], axis=0
     ).astype(jnp.bfloat16)
-    for c in range(CHUNKS):
-        weight = weights[:, c * LANES : (c + 1) * LANES]
-        for k in range(2):
-            weighted = visibility[:, k, c * LANES : (c + 1) * LANES] * weight
-            at = (k * CHUNKS + c) * PITCH
-            placed[at : at + CAP * dests, :] = jnp.dot(
-                choose, weighted.astype(jnp.bfloat16), preferred_element_type=jnp.float32
-            )
     rest = coords[...]
     pieces = []
     for _ in range(3):
@@ -290,6 +290,16 @@
         ]
         halves.append((sides[0] + sides[1]).astype(jnp.bfloat16))
 
+    copies[1].wait()
+    copies[0].wait()
+    for c in range(CHUNKS):
+        weight = weights[:, c * LANES : (c + 1) * LANES]
+        for k in range(2):
+            weighted = visibility[:, k, c * LANES : (c + 1) * LANES] * weight
+            at = (k * CHUNKS + c) * PITCH
+            placed[at : at + CAP * dests, :] = jnp.dot(
+                choose, weighted.astype(jnp.bfloat16), preferred_element_type=jnp.float32
+            )
     def write(i, carry):
         for h in range(2):
             d = 2 * i + h
@@ -310,16 +320,7 @@
     turn_x = np.zeros((2, SUB, LANES), np.float32)
     for k in range(2):
         turn_x[k, PERM_X, k * SUB + np.arange(SUB)] = 1.0
-    vmem = pl.BlockSpec(memory_space=pltpu.VMEM)
-    return pl.pallas_call(
-        pack_kernel,
-        out_shape=jax.ShapeDtypeStruct((grid_count, MSG_ROWS, LANES), jnp.bfloat16),
-        in_specs=[vmem] * 8,
-        out_specs=vmem,
-        scratch_shapes=[pltpu.VMEM((SLOT_ROWS * PITCH, LANES), jnp.float32)],
-        compiler_params=pltpu.CompilerParams(vmem_limit_bytes=40 * 1024 * 1024),
-        name="pack_blocks",
-    )(
+    operands = [
         visibility,
         weights,
         block_uv.transpose(1, 2, 0).reshape(2 * TS, blocks),
@@ -328,7 +329,18 @@
         screen,
         jnp.asarray(turn_y, jnp.bfloat16),
         jnp.asarray(turn_x, jnp.bfloat16),
-    )
+    ]
+    return pl.pallas_call(
+        pack_kernel,
+        out_shape=jax.ShapeDtypeStruct((grid_count, MSG_ROWS, LANES), jnp.bfloat16),
+        in_specs=[pl.BlockSpec(memory_space=pltpu.HBM)] * 8,
+        out_specs=pl.BlockSpec(memory_space=pltpu.VMEM),
+        scratch_shapes=[pltpu.VMEM((SLOT_ROWS * PITCH, LANES), jnp.float32)]
+        + [pltpu.VMEM(x.shape, x.dtype) for x in operands]
+        + [pltpu.SemaphoreType.DMA((8,))],
+        compiler_params=pltpu.CompilerParams(vmem_limit_bytes=56 * 1024 * 1024),
+        name="pack_blocks",
+    )(*operands)
 
 
 def gridded(tags, recv, other, scale, bands):
@@ -337,7 +349,7 @@
     vmem = pl.BlockSpec(memory_space=pltpu.VMEM)
     return pl.pallas_call(
         grid_kernel,
-        out_shape=jax.ShapeDtypeStruct((bands, SG_DEV, SUB // bands, LANES), jnp.float32),
+        out_shape=jax.ShapeDtypeStruct((bands, SUB // bands, SG_DEV, LANES), jnp.float32),
         in_specs=[pl.BlockSpec(memory_space=pltpu.SMEM)] + [vmem] * 7,
         out_specs=vmem,
         scratch_shapes=[
@@ -382,7 +394,7 @@
     scale = jnp.tile(chan_ratio[0] * (math.pi / SUB), 2 * TS)[None, :]
     rows = gridded(tags, recv, other, scale, bands)
     parts = lax.all_to_all(rows, "band", split_axis=0, concat_axis=0, tiled=True)
-    return jnp.transpose(jnp.sum(parts, axis=0), (1, 0, 2))
+    return jnp.sum(parts, axis=0)
 
 
 def solution(mesh):

time: 87.1 us -> 84.5 us (0.970)
  local copies, waits for them, and re-layouts: 6.24 us -> 0.75 us
  Pallas kernels: 17.4 us -> 19.7 us
    unnamed x26 -> x10, local copies, waits for them, and re-layouts: 4.86 us -> 0.03 us
    pallas_call x1, Pallas kernels: 0.9 us -> 3.12 us  [packed(): pl.pallas_call(pack_kernel, out_shape=jax.ShapeDtypeStruct((grid_count, M...]
where the time goes in v3:
time: 84.5 us; the launch traced here: 84.3 us
  blocking collectives  59.9 us (71%)
  Pallas kernels  19.7 us (23%)
  starting transfers between devices  1.92 us (2%)
  waiting for transfers between devices  1.21 us (1%)
    all_to_all x1, blocking collectives, shards(): lax.all_to_all(message, 'grid', split_axis=0, concat_axis=0, tiled=True)  48.8 us
    pallas_call x1, Pallas kernels, gridded(): pl.pallas_call(grid_kernel, out_shape=jax.ShapeDtypeStruct((bands, SUB //...  16.6 us
    all_to_all x1, blocking collectives, shards(): lax.all_to_all(rows, 'band', split_axis=0, concat_axis=0, tiled=True)  11.1 us
    pallas_call x1, Pallas kernels, packed(): pl.pallas_call(pack_kernel, out_shape=jax.ShapeDtypeStruct((grid_count, M...  3.12 us
    ppermute x1, starting transfers between devices, shards(): lax.ppermute(recv[:, CAP * SLOT_ROWS:], 'grid', [(i, i ^ 1) for i in rang...  1.92 us
  transfers between devices with their start and end apart: 1, of which 1 were waited for; matrix products, arithmetic and copies ran while one was open for 1% of the time, Pallas kernels for 0%

profile of v3, /device:TPU:8, one launch (start us, length us, event | category | flops | bytes accessed | tf_op | source)
XLA Modules:
  0.0 84.3 jit_solution(7465956656586223412)
XLA Ops:
  0.0 3.1 %pack_blocks.1 = bf16[128,32,128]{2,1,0:T(8,128)(2,1)} custom-call(f32[128,2,384]{2,1,0:T(2,128)} %bitcast.13, f32[128,384]{1,0:T(8,128)} %bitcast.14, f32[32,128]{1,0:T(8,128)} %bitcast.15, s32[1,128]{1,0:T(1,128)} %refs_3_.1, s32[2,128]{1,0:T(2,128)} %bitcast.17, bf16[64,64]{1,0:T(8,128)(2,1)} %bitcast.16, bf16[64,64]{1,0:T(8,128)(2,1)} %constant.16.clone.refs_6_, ...), custom_call_target="tpu_custom_call" | custom-call | tf_op jit(solution)/shard_map/pack_blocks/pallas_call | solution.py:333
  3.1 48.8 %all_to_all.10.recv = bf16[128,32,128]{2,1,0:T(8,128)(2,1)S(1)} all-to-all(bf16[128,32,128]{2,1,0:T(8,128)(2,1)} %pack_blocks.1), channel_id=1, replica_groups=mesh['grid'=128,'band'=4] {'grid'}, dimensions={0} | all-to-all | bytes 2097152 | tf_op jit(solution)/shard_map/all_to_all | solution.py:385
  52.0 0.2 fusion
  52.2 0.0 copy-start.4
  52.2 1.9 %collective-permute-start = (bf16[128,16,128]{2,1,0:T(8,128)(2,1)S(1)}, bf16[128,16,128]{2,1,0:T(8,128)(2,1)S(1)}, u32[]{:S(2)}, u32[]{:S(2)}) collective-permute-start(bf16[128,16,128]{2,1,0:T(8,128)(2,1)S(1)} %get-tuple-element.5), channel_id=1, source_target_pairs={{0,4},{4,0},{8,12},{12,8},{16,20},{20,16},{24,28},{28,24},{32,36},... | collective-permute-start | bytes 1572872 | tf_op jit(solution)/shard_map/ppermute | solution.py:386
  54.1 0.0 copy-done.4
  54.1 0.1 broadcast_in_dim_tile.3.scale
  54.2 0.3 slice.13
  54.5 0.0 copy-start
  54.5 0.0 copy-start.3
  54.5 0.0 copy-start.1
  54.5 0.0 copy-start.2
  54.6 0.2 reshape.12.tags
  54.8 1.2 %collective-permute-done.other = bf16[128,16,128]{2,1,0:T(8,128)(2,1)S(1)} collective-permute-done((bf16[128,16,128]{2,1,0:T(8,128)(2,1)S(1)}, bf16[128,16,128]{2,1,0:T(8,128)(2,1)S(1)}, u32[]{:S(2)}, u32[]{:S(2)}) %collective-permute-start) | collective-permute-done | bytes 524320 | tf_op jit(solution)/shard_map/ppermute | solution.py:386
  56.0 0.0 copy-done
  56.0 0.0 copy-done.3
  56.0 0.0 copy-done.1
  56.0 0.0 copy-done.2
  56.0 16.6 %grid_blocks.1 = f32[4,16,8,128]{3,2,1,0:T(8,128)S(1)} custom-call(s32[768]{0:T(1024)S(1)} %reshape.12.tags, bf16[128,32,128]{2,1,0:T(8,128)(2,1)S(1)} %all_to_all.10.recv, bf16[128,16,128]{2,1,0:T(8,128)(2,1)S(1)} %collective-permute-done.other, f32[1,768]{1,0:T(1,128)S(1)} %broadcast_in_dim_tile.3.scale, bf16[128,768]{1,0:T(8,128)(2,1)S(1)} %copy-done, ...), custom_call_target="tpu_custom_call" | custom-call | tf_op jit(solution)/shard_map/grid_blocks/pallas_call | solution.py:350
  72.6 11.1 %all_to_all.11 = f32[4,16,8,128]{3,2,1,0:T(8,128)S(1)} all-to-all(f32[4,16,8,128]{3,2,1,0:T(8,128)S(1)} %grid_blocks.1), channel_id=1, replica_groups=mesh['grid'=128,'band'=4] {'band'}, dimensions={0} | all-to-all | bytes 524288 | tf_op jit(solution)/shard_map/all_to_all | solution.py:396
  83.6 0.6 reduce_sum.9
  (3 shorter events, 0.0 us)
Async XLA Ops:
  52.2 1.9 %copy-start.4 = (f32[1,24]{1,0:T(1,128)S(1)}, f32[1,24]{1,0:T(1,128)}, u32[]{:S(2)}) copy-start(f32[1,24]{1,0:T(1,128)} %param.16) | copy-start | bytes 292
  52.2 3.8 %collective-permute-start = (bf16[128,16,128]{2,1,0:T(8,128)(2,1)S(1)}, bf16[128,16,128]{2,1,0:T(8,128)(2,1)S(1)}, u32[]{:S(2)}, u32[]{:S(2)}) collective-permute-start(bf16[128,16,128]{2,1,0:T(8,128)(2,1)S(1)} %get-tuple-element.5), channel_id=1, source_target_pairs={{0,4},{4,0},{8,12},{12,8},{16,20},{20,16},{24,28},{28,24},{32,36},... | collective-permute-start | bytes 1572872 | tf_op jit(solution)/shard_map/ppermute | solution.py:386
  54.5 1.5 %copy-start = (bf16[128,768]{1,0:T(8,128)(2,1)S(1)}, bf16[128,768]{1,0:T(8,128)(2,1)}, u32[]{:S(2)}) copy-start(bf16[128,768]{1,0:T(8,128)(2,1)} %constant.18.clone.spread) | copy-start | bytes 589828
  54.5 1.5 %copy-start.3 = (f32[64,128]{1,0:T(8,128)S(1)}, f32[64,128]{1,0:T(8,128)}, u32[]{:S(2)}) copy-start(f32[64,128]{1,0:T(8,128)} %constant.19.clone.window) | copy-start | bytes 98308
  54.5 1.5 %copy-start.1 = (f32[128,128]{1,0:T(8,128)S(1)}, f32[128,128]{1,0:T(8,128)}, u32[]{:S(2)}) copy-start(f32[128,128]{1,0:T(8,128)} %constant.20.clone.across_dft) | copy-start | bytes 196612
  54.5 1.4 %copy-start.2 = (f32[128,128]{1,0:T(8,128)S(1)}, f32[128,128]{1,0:T(8,128)}, u32[]{:S(2)}) copy-start(f32[128,128]{1,0:T(8,128)} %constant.21.clone.down_dft) | copy-start | bytes 196612

commit v4 on v3

--- a/solution.py
+++ b/solution.py
@@ -2,6 +2,7 @@
 
 import jax
 import jax.numpy as jnp
+import ml_dtypes
 import numpy as np
 from jax import lax
 from jax.experimental import pallas as pl
@@ -37,12 +38,15 @@
 
     def real_form(perm):
         part = dft[:, perm].T
-        return np.block([[part.real, part.imag], [-part.imag, part.real]])
+        form = np.block([[part.real, part.imag], [-part.imag, part.real]]).astype(np.float32)
+        high = form.astype(ml_dtypes.bfloat16)
+        low = (form - high.astype(np.float32)).astype(ml_dtypes.bfloat16)
+        return np.concatenate([high, high, low], axis=0)
 
     return (
         window.astype(np.float32),
-        real_form(PERM_X).astype(np.float32),
-        real_form(PERM_Y).astype(np.float32),
+        real_form(PERM_X),
+        real_form(PERM_Y),
     )
 
 
@@ -58,17 +62,17 @@
 def sincos(angle):
     square = angle * angle
     sine = angle * (
-        1.0
+        0.999999987111644
+        + square
+        * (-0.16666619937913615 + square * (0.008330684107237122 + square * -0.00019359740077908407))
+    )
+    cosine = 0.999999999715393 + square * (
+        -0.49999998388310446
         + square
         * (
-            -1.0 / 6
-            + square * (1.0 / 120 + square * (-1.0 / 5040 + square * (1.0 / 362880)))
+            0.04166652058451844
+            + square * (-0.0013884251197818648 + square * 2.4199524865236834e-05)
         )
-    )
-    cosine = 1.0 + square * (
-        -0.5
-        + square
-        * (1.0 / 24 + square * (-1.0 / 720 + square * (1.0 / 40320 + square * (-1.0 / 3628800))))
     )
     return cosine, sine
 
@@ -218,23 +222,31 @@
         return carry
 
     lax.fori_loop(0, turns, turn, 0)
-    exact = lax.Precision.HIGHEST
     tapered = (total[...] * window[...]).reshape(SG_DEV * SUB, LANES)
-    first = jnp.dot(tapered, across_dft[...], precision=exact, preferred_element_type=jnp.float32)
+    high, low_part = pieces_of(tapered)
+    first = jnp.dot(
+        jnp.concatenate([high, low_part, high], axis=1),
+        across_dft[...],
+        preferred_element_type=jnp.float32,
+    )
     bands = out.shape[0]
     each = SUB // bands
     for g in range(SG_DEV):
         mine = first[g * SUB : (g + 1) * SUB]
-        stacked = jnp.concatenate([mine[:, :SUB], mine[:, SUB:]], axis=0)
-        second = lax.dot_general(
-            stacked,
+        stacked = jnp.concatenate([mine[:, :SUB], mine[:, SUB:]], axis=0).T
+        high, low_part = pieces_of(stacked)
+        second = jnp.dot(
+            jnp.concatenate([high, low_part, high], axis=1),
             down_dft[...],
-            (((0,), (0,)), ((), ())),
-            precision=exact,
             preferred_element_type=jnp.float32,
         )
         for b in range(bands):
             out[b, :, g, :] = second[b * each : (b + 1) * each]
+
+
+def pieces_of(value):
+    high = value.astype(jnp.bfloat16)
+    return high, (value - high.astype(jnp.float32)).astype(jnp.bfloat16)
 
 
 def pack_kernel(*refs):

time: 84.5 us -> 83.4 us (0.987)
  Pallas kernels: 19.7 us -> 18.5 us
    pallas_call x1, Pallas kernels: 16.6 us -> 15.4 us  [gridded(): pl.pallas_call(grid_kernel, out_shape=jax.ShapeDtypeStruct((bands, SUB //...]
where the time goes in v4:
time: 83.4 us; the launch traced here: 83.1 us
  blocking collectives  59.9 us (72%)
  Pallas kernels  18.5 us (22%)
  starting transfers between devices  1.92 us (2%)
  waiting for transfers between devices  1.22 us (1%)
    all_to_all x1, blocking collectives, shards(): lax.all_to_all(message, 'grid', split_axis=0, concat_axis=0, tiled=True)  48.8 us
    pallas_call x1, Pallas kernels, gridded(): pl.pallas_call(grid_kernel, out_shape=jax.ShapeDtypeStruct((bands, SUB //...  15.4 us
    all_to_all x1, blocking collectives, shards(): lax.all_to_all(rows, 'band', split_axis=0, concat_axis=0, tiled=True)  11.1 us
    pallas_call x1, Pallas kernels, packed(): pl.pallas_call(pack_kernel, out_shape=jax.ShapeDtypeStruct((grid_count, M...  3.12 us
    ppermute x1, starting transfers between devices, shards(): lax.ppermute(recv[:, CAP * SLOT_ROWS:], 'grid', [(i, i ^ 1) for i in rang...  1.92 us
  transfers between devices with their start and end apart: 1, of which 1 were waited for; matrix products, arithmetic and copies ran while one was open for 1% of the time, Pallas kernels for 0%

profile of v4, /device:TPU:8, one launch (start us, length us, event | category | flops | bytes accessed | tf_op | source)
XLA Modules:
  0.0 83.1 jit_solution(2632715705373431236)
XLA Ops:
  0.0 3.1 %pack_blocks.1 = bf16[128,32,128]{2,1,0:T(8,128)(2,1)} custom-call(f32[128,2,384]{2,1,0:T(2,128)} %bitcast.13, f32[128,384]{1,0:T(8,128)} %bitcast.14, f32[32,128]{1,0:T(8,128)} %bitcast.15, s32[1,128]{1,0:T(1,128)} %refs_3_.1, s32[2,128]{1,0:T(2,128)} %bitcast.17, bf16[64,64]{1,0:T(8,128)(2,1)} %bitcast.16, bf16[64,64]{1,0:T(8,128)(2,1)} %constant.16.clone.refs_6_, ...), custom_call_target="tpu_custom_call" | custom-call | tf_op jit(solution)/shard_map/pack_blocks/pallas_call | solution.py:345
  3.1 48.8 %all_to_all.10.recv = bf16[128,32,128]{2,1,0:T(8,128)(2,1)S(1)} all-to-all(bf16[128,32,128]{2,1,0:T(8,128)(2,1)} %pack_blocks.1), channel_id=1, replica_groups=mesh['grid'=128,'band'=4] {'grid'}, dimensions={0} | all-to-all | bytes 2097152 | tf_op jit(solution)/shard_map/all_to_all | solution.py:397
  52.0 0.2 fusion
  52.2 0.0 copy-start.4
  52.2 1.9 %collective-permute-start = (bf16[128,16,128]{2,1,0:T(8,128)(2,1)S(1)}, bf16[128,16,128]{2,1,0:T(8,128)(2,1)S(1)}, u32[]{:S(2)}, u32[]{:S(2)}) collective-permute-start(bf16[128,16,128]{2,1,0:T(8,128)(2,1)S(1)} %get-tuple-element.5), channel_id=1, source_target_pairs={{0,4},{4,0},{8,12},{12,8},{16,20},{20,16},{24,28},{28,24},{32,36},... | collective-permute-start | bytes 1572872 | tf_op jit(solution)/shard_map/ppermute | solution.py:398
  54.1 0.0 copy-done.4
  54.1 0.1 broadcast_in_dim_tile.3.scale
  54.2 0.0 copy-start.3
  54.2 0.3 slice.13
  54.5 0.0 copy-start
  54.5 0.0 copy-start.2
  54.5 0.0 copy-start.1
  54.5 0.2 reshape.12.tags
  54.8 1.2 %collective-permute-done.other = bf16[128,16,128]{2,1,0:T(8,128)(2,1)S(1)} collective-permute-done((bf16[128,16,128]{2,1,0:T(8,128)(2,1)S(1)}, bf16[128,16,128]{2,1,0:T(8,128)(2,1)S(1)}, u32[]{:S(2)}, u32[]{:S(2)}) %collective-permute-start) | collective-permute-done | bytes 524320 | tf_op jit(solution)/shard_map/ppermute | solution.py:398
  56.0 0.0 copy-done.3
  56.0 0.0 copy-done
  56.0 0.0 copy-done.2
  56.0 0.0 copy-done.1
  56.0 15.4 %grid_blocks.1 = f32[4,16,8,128]{3,2,1,0:T(8,128)S(1)} custom-call(s32[768]{0:T(1024)S(1)} %reshape.12.tags, bf16[128,32,128]{2,1,0:T(8,128)(2,1)S(1)} %all_to_all.10.recv, bf16[128,16,128]{2,1,0:T(8,128)(2,1)S(1)} %collective-permute-done.other, f32[1,768]{1,0:T(1,128)S(1)} %broadcast_in_dim_tile.3.scale, bf16[128,768]{1,0:T(8,128)(2,1)S(1)} %copy-done, ...), custom_call_target="tpu_custom_call" | custom-call | tf_op jit(solution)/shard_map/grid_blocks/pallas_call | solution.py:362
  71.4 11.1 %all_to_all.11 = f32[4,16,8,128]{3,2,1,0:T(8,128)S(1)} all-to-all(f32[4,16,8,128]{3,2,1,0:T(8,128)S(1)} %grid_blocks.1), channel_id=1, replica_groups=mesh['grid'=128,'band'=4] {'band'}, dimensions={0} | all-to-all | bytes 524288 | tf_op jit(solution)/shard_map/all_to_all | solution.py:408
  82.5 0.6 reduce_sum.9
  (3 shorter events, 0.0 us)
Async XLA Ops:
  52.2 1.9 %copy-start.4 = (f32[1,24]{1,0:T(1,128)S(1)}, f32[1,24]{1,0:T(1,128)}, u32[]{:S(2)}) copy-start(f32[1,24]{1,0:T(1,128)} %param.16) | copy-start | bytes 292
  52.2 3.8 %collective-permute-start = (bf16[128,16,128]{2,1,0:T(8,128)(2,1)S(1)}, bf16[128,16,128]{2,1,0:T(8,128)(2,1)S(1)}, u32[]{:S(2)}, u32[]{:S(2)}) collective-permute-start(bf16[128,16,128]{2,1,0:T(8,128)(2,1)S(1)} %get-tuple-element.5), channel_id=1, source_target_pairs={{0,4},{4,0},{8,12},{12,8},{16,20},{20,16},{24,28},{28,24},{32,36},... | collective-permute-start | bytes 1572872 | tf_op jit(solution)/shard_map/ppermute | solution.py:398
  54.2 1.8 %copy-start.3 = (f32[64,128]{1,0:T(8,128)S(1)}, f32[64,128]{1,0:T(8,128)}, u32[]{:S(2)}) copy-start(f32[64,128]{1,0:T(8,128)} %constant.19.clone.window) | copy-start | bytes 98308
  54.5 1.5 %copy-start = (bf16[128,768]{1,0:T(8,128)(2,1)S(1)}, bf16[128,768]{1,0:T(8,128)(2,1)}, u32[]{:S(2)}) copy-start(bf16[128,768]{1,0:T(8,128)(2,1)} %constant.18.clone.spread) | copy-start | bytes 589828
  54.5 1.5 %copy-start.2 = (bf16[384,128]{1,0:T(8,128)(2,1)S(1)}, bf16[384,128]{1,0:T(8,128)(2,1)}, u32[]{:S(2)}) copy-start(bf16[384,128]{1,0:T(8,128)(2,1)} %constant.21.clone.down_dft) | copy-start | bytes 294916
  54.5 1.4 %copy-start.1 = (bf16[384,128]{1,0:T(8,128)(2,1)S(1)}, bf16[384,128]{1,0:T(8,128)(2,1)}, u32[]{:S(2)}) copy-start(bf16[384,128]{1,0:T(8,128)(2,1)} %constant.20.clone.across_dft) | copy-start | bytes 294916

commit v5 on v4

--- a/solution.py
+++ b/solution.py
@@ -106,6 +106,7 @@
     angles,
     beams,
     total,
+    ordered_rows,
     *buffers,
 ):
     sources = recv.shape[0]
@@ -229,8 +230,6 @@
         across_dft[...],
         preferred_element_type=jnp.float32,
     )
-    bands = out.shape[0]
-    each = SUB // bands
     for g in range(SG_DEV):
         mine = first[g * SUB : (g + 1) * SUB]
         stacked = jnp.concatenate([mine[:, :SUB], mine[:, SUB:]], axis=0).T
@@ -240,8 +239,8 @@
             down_dft[...],
             preferred_element_type=jnp.float32,
         )
-        for b in range(bands):
-            out[b, :, g, :] = second[b * each : (b + 1) * each]
+        ordered_rows[:, g, :] = second
+    out[...] = ordered_rows[...].reshape(out.shape).astype(out.dtype)
 
 
 def pieces_of(value):
@@ -361,7 +360,7 @@
     vmem = pl.BlockSpec(memory_space=pltpu.VMEM)
     return pl.pallas_call(
         grid_kernel,
-        out_shape=jax.ShapeDtypeStruct((bands, SUB // bands, SG_DEV, LANES), jnp.float32),
+        out_shape=jax.ShapeDtypeStruct((bands, SUB // bands * SG_DEV, LANES), jnp.bfloat16),
         in_specs=[pl.BlockSpec(memory_space=pltpu.SMEM)] + [vmem] * 7,
         out_specs=vmem,
         scratch_shapes=[
@@ -369,6 +368,7 @@
             pltpu.VMEM((slots, 2 * VIS), jnp.float32),
             pltpu.VMEM((recv.shape[0], SUB, LANES), jnp.float32),
             pltpu.VMEM((SG_DEV, SUB, LANES), jnp.float32),
+            pltpu.VMEM((SUB, SG_DEV, LANES), jnp.float32),
             pltpu.VMEM((12 * CHUNKS, 8, LANES), jnp.float32),
             pltpu.VMEM((4 * CHUNKS * 64, LANES), jnp.float32),
             pltpu.VMEM((12 * CHUNKS, 8, LANES), jnp.float32),
@@ -406,7 +406,8 @@
     scale = jnp.tile(chan_ratio[0] * (math.pi / SUB), 2 * TS)[None, :]
     rows = gridded(tags, recv, other, scale, bands)
     parts = lax.all_to_all(rows, "band", split_axis=0, concat_axis=0, tiled=True)
-    return jnp.sum(parts, axis=0)
+    total = jnp.sum(parts.astype(jnp.float32), axis=0)
+    return total.reshape(SUB // bands, SG_DEV, LANES)
 
 
 def solution(mesh):

time: 83.4 us -> 82.4 us (0.988)
  blocking collectives: 59.9 us -> 58.9 us
    all_to_all x1, blocking collectives: 11.1 us -> 10.1 us  [shards(): lax.all_to_all(rows, 'band', split_axis=0, concat_axis=0, tiled=True)]
where the time goes in v5:
time: 82.4 us; the launch traced here: 82.2 us
  blocking collectives  58.9 us (71%)
  Pallas kernels  18.6 us (23%)
  starting transfers between devices  1.92 us (2%)
  waiting for transfers between devices  1.22 us (1%)
    all_to_all x1, blocking collectives, shards(): lax.all_to_all(message, 'grid', split_axis=0, concat_axis=0, tiled=True)  48.8 us
    pallas_call x1, Pallas kernels, gridded(): pl.pallas_call(grid_kernel, out_shape=jax.ShapeDtypeStruct((bands, SUB //...  15.4 us
    all_to_all x1, blocking collectives, shards(): lax.all_to_all(rows, 'band', split_axis=0, concat_axis=0, tiled=True)  10.1 us
    pallas_call x1, Pallas kernels, packed(): pl.pallas_call(pack_kernel, out_shape=jax.ShapeDtypeStruct((grid_count, M...  3.12 us
    ppermute x1, starting transfers between devices, shards(): lax.ppermute(recv[:, CAP * SLOT_ROWS:], 'grid', [(i, i ^ 1) for i in rang...  1.92 us
  transfers between devices with their start and end apart: 1, of which 1 were waited for; matrix products, arithmetic and copies ran while one was open for 1% of the time, Pallas kernels for 0%

profile of v5, /device:TPU:8, one launch (start us, length us, event | category | flops | bytes accessed | tf_op | source)
XLA Modules:
  0.0 82.2 jit_solution(15392207170701153306)
XLA Ops:
  0.0 3.1 %pack_blocks.1 = bf16[128,32,128]{2,1,0:T(8,128)(2,1)} custom-call(f32[128,2,384]{2,1,0:T(2,128)} %bitcast.14, f32[128,384]{1,0:T(8,128)} %bitcast.15, f32[32,128]{1,0:T(8,128)} %bitcast.16, s32[1,128]{1,0:T(1,128)} %refs_3_.1, s32[2,128]{1,0:T(2,128)} %bitcast.18, bf16[64,64]{1,0:T(8,128)(2,1)} %bitcast.17, bf16[64,64]{1,0:T(8,128)(2,1)} %constant.16.clone.refs_6_, ...), custom_call_target="tpu_custom_call" | custom-call | tf_op jit(solution)/shard_map/pack_blocks/pallas_call | solution.py:344
  3.1 48.8 %all_to_all.10.recv = bf16[128,32,128]{2,1,0:T(8,128)(2,1)S(1)} all-to-all(bf16[128,32,128]{2,1,0:T(8,128)(2,1)} %pack_blocks.1), channel_id=1, replica_groups=mesh['grid'=128,'band'=4] {'grid'}, dimensions={0} | all-to-all | bytes 2097152 | tf_op jit(solution)/shard_map/all_to_all | solution.py:397
  52.0 0.2 fusion
  52.2 0.0 copy-start.4
  52.2 1.9 %collective-permute-start = (bf16[128,16,128]{2,1,0:T(8,128)(2,1)S(1)}, bf16[128,16,128]{2,1,0:T(8,128)(2,1)S(1)}, u32[]{:S(2)}, u32[]{:S(2)}) collective-permute-start(bf16[128,16,128]{2,1,0:T(8,128)(2,1)S(1)} %get-tuple-element.5), channel_id=1, source_target_pairs={{0,4},{4,0},{8,12},{12,8},{16,20},{20,16},{24,28},{28,24},{32,36},... | collective-permute-start | bytes 1572872 | tf_op jit(solution)/shard_map/ppermute | solution.py:398
  54.1 0.0 copy-done.4
  54.1 0.1 broadcast_in_dim_tile.3.scale
  54.2 0.0 copy-start.3
  54.2 0.3 slice.13
  54.5 0.0 copy-start
  54.5 0.0 copy-start.2
  54.5 0.0 copy-start.1
  54.5 0.2 reshape.16.tags
  54.8 1.2 %collective-permute-done.other = bf16[128,16,128]{2,1,0:T(8,128)(2,1)S(1)} collective-permute-done((bf16[128,16,128]{2,1,0:T(8,128)(2,1)S(1)}, bf16[128,16,128]{2,1,0:T(8,128)(2,1)S(1)}, u32[]{:S(2)}, u32[]{:S(2)}) %collective-permute-start) | collective-permute-done | bytes 524320 | tf_op jit(solution)/shard_map/ppermute | solution.py:398
  56.0 0.0 copy-done.3
  56.0 0.0 copy-done
  56.0 0.0 copy-done.2
  56.0 0.0 copy-done.1
  56.0 15.4 %grid_blocks.1 = bf16[4,128,128]{2,1,0:T(8,128)(2,1)S(1)} custom-call(s32[768]{0:T(1024)S(1)} %reshape.16.tags, bf16[128,32,128]{2,1,0:T(8,128)(2,1)S(1)} %all_to_all.10.recv, bf16[128,16,128]{2,1,0:T(8,128)(2,1)S(1)} %collective-permute-done.other, f32[1,768]{1,0:T(1,128)S(1)} %broadcast_in_dim_tile.3.scale, bf16[128,768]{1,0:T(8,128)(2,1)S(1)} %copy-done, ...), custom_call_target="tpu_custom_call" | custom-call | tf_op jit(solution)/shard_map/grid_blocks/pallas_call | solution.py:361
  71.4 10.1 %all_to_all.11 = bf16[4,128,128]{2,1,0:T(8,128)(2,1)S(1)} all-to-all(bf16[4,128,128]{2,1,0:T(8,128)(2,1)S(1)} %grid_blocks.1), channel_id=1, replica_groups=mesh['grid'=128,'band'=4] {'band'}, dimensions={0} | all-to-all | bytes 262144 | tf_op jit(solution)/shard_map/all_to_all | solution.py:408
  81.5 0.6 convert_reduce_fusion
  (3 shorter events, 0.0 us)
Async XLA Ops:
  52.2 1.9 %copy-start.4 = (f32[1,24]{1,0:T(1,128)S(1)}, f32[1,24]{1,0:T(1,128)}, u32[]{:S(2)}) copy-start(f32[1,24]{1,0:T(1,128)} %param.16) | copy-start | bytes 292
  52.2 3.8 %collective-permute-start = (bf16[128,16,128]{2,1,0:T(8,128)(2,1)S(1)}, bf16[128,16,128]{2,1,0:T(8,128)(2,1)S(1)}, u32[]{:S(2)}, u32[]{:S(2)}) collective-permute-start(bf16[128,16,128]{2,1,0:T(8,128)(2,1)S(1)} %get-tuple-element.5), channel_id=1, source_target_pairs={{0,4},{4,0},{8,12},{12,8},{16,20},{20,16},{24,28},{28,24},{32,36},... | collective-permute-start | bytes 1572872 | tf_op jit(solution)/shard_map/ppermute | solution.py:398
  54.2 1.8 %copy-start.3 = (f32[64,128]{1,0:T(8,128)S(1)}, f32[64,128]{1,0:T(8,128)}, u32[]{:S(2)}) copy-start(f32[64,128]{1,0:T(8,128)} %constant.19.clone.window) | copy-start | bytes 98308
  54.5 1.5 %copy-start = (bf16[128,768]{1,0:T(8,128)(2,1)S(1)}, bf16[128,768]{1,0:T(8,128)(2,1)}, u32[]{:S(2)}) copy-start(bf16[128,768]{1,0:T(8,128)(2,1)} %constant.18.clone.spread) | copy-start | bytes 589828
  54.5 1.5 %copy-start.2 = (bf16[384,128]{1,0:T(8,128)(2,1)S(1)}, bf16[384,128]{1,0:T(8,128)(2,1)}, u32[]{:S(2)}) copy-start(bf16[384,128]{1,0:T(8,128)(2,1)} %constant.21.clone.down_dft) | copy-start | bytes 294916
  54.5 1.4 %copy-start.1 = (bf16[384,128]{1,0:T(8,128)(2,1)S(1)}, bf16[384,128]{1,0:T(8,128)(2,1)}, u32[]{:S(2)}) copy-start(bf16[384,128]{1,0:T(8,128)(2,1)} %constant.20.clone.across_dft) | copy-start | bytes 294916
